TPU v7x, 512 devices: a whole 4x4x16 slice. The times are simulated.
512 devices in a mesh: dp: 16 (over z), work: 32 (over y, x, core).
Axes of the slice: x: 4, y: 4, z: 16, core: 2. Of those that a mesh axis runs over, the one named last changes fastest.
Arguments:
- grads: bfloat16 [16, 8192, 4096], P('dp', None, 'work')
- worker_list: int32 [16, 8, 2], P('dp'), may hold values from 0 to 3
Outputs:
- update: bfloat16 [8192, 4096], P('dp', 'work')
- worker_roots: bfloat16 [16, 32, 2, 512, 512], P('dp', 'work')
Inputs may be any that keep to these rules, and one draw needn't show every extreme that they name: `worker_list`: each factor of each block has exactly one worker, among the four work devices that hold the block's columns.
All inputs are finite; a program needn't handle non-finite values.
Results may differ from a plain program's by a relative error of at most 0.039.
Values may be sent and summed in bfloat16 or wider, within the bound.
No kernel may reach another device: no remote copies, remote signals or barrier semaphores. Data moves between devices by JAX's collectives and lax.ppermute only.
A program may use at most 64 MiB of HBM per device.

v0:
```python
import jax
import jax.numpy as jnp
from jax import lax
from jax.sharding import PartitionSpec as P

ITERS = 3


def from_partner(value, axis, distance):
    return lax.ppermute(value, axis, [(i, i ^ 1 << distance) for i in range(lax.axis_size(axis))])


def for_sending(value):
    return jax.tree.map(lambda a: a.astype(jnp.bfloat16) if a.dtype == jnp.float32 else a, value)


def batched(left, right):
    return jnp.einsum("sij,sjk->sik", left, right, preferred_element_type=jnp.float32)


def gram_matrix(operand, contract):
    return lax.dot_general(
        operand, operand, (((contract,), (contract,)), ((), ())), preferred_element_type=jnp.float32
    )


def newton_roots(stats):
    order = stats.shape[-1]
    identity = jnp.eye(order, dtype=jnp.float32)
    damp = 0.1 * (jnp.trace(stats, axis1=1, axis2=2) / order + 1e-06)
    damped = stats + damp[:, None, None] * identity
    scale = jnp.sqrt(jnp.sum(damped * damped, axis=(1, 2)) + 1e-06) * 0.25
    current = damped / scale[:, None, None]
    iterate = jnp.broadcast_to(identity, stats.shape)
    for step in range(ITERS):
        factor = ((5.0 * identity - current) * 0.25).astype(jnp.bfloat16)
        square = batched(factor, factor).astype(jnp.bfloat16)
        fourth = batched(square, square).astype(jnp.bfloat16)
        current = batched(fourth, current.astype(jnp.bfloat16))
        iterate = batched(iterate.astype(jnp.bfloat16), factor)
    return (iterate * (scale ** (-0.25))[:, None, None]).astype(jnp.bfloat16)


def local(grads, worker_list):
    summed = lax.psum_scatter(
        grads[0].astype(jnp.float32).astype(jnp.bfloat16), "dp", scatter_dimension=0, tiled=True
    )
    width = summed.shape[1]
    index = lax.axis_index("work")
    place = index % 4
    block = summed
    for level in range(2):
        other = from_partner(block, "work", level)
        lower = index // (1 << level) % 2 == 0
        block = jnp.where(
            lower, jnp.concatenate([block, other], 1), jnp.concatenate([other, block], 1)
        )
    assigned = lax.dynamic_index_in_dim(worker_list[0], index // 4, 0, keepdims=False)
    mine = assigned == place
    chosen = mine[:, None, None]
    nothing = jnp.zeros((), jnp.bfloat16)
    order = block.shape[0]

    def none_listed(operand):
        return jnp.zeros((2, order, order), jnp.bfloat16)

    def one_listed(operand):
        picked = jnp.where(mine[0], operand, operand.T)
        single = newton_roots(gram_matrix(picked, 1)[None])[0]
        return jnp.where(chosen, single[None], nothing)

    def both_listed(operand):
        return newton_roots(jnp.stack([gram_matrix(operand, 1), gram_matrix(operand, 0)]))

    count = jnp.sum(mine.astype(jnp.int32))
    held = lax.switch(count, [none_listed, one_listed, both_listed], block)
    shared = held
    for level in range(2):
        shared = shared + jax.tree.map(
            lambda part, own: part.astype(own.dtype),
            from_partner(for_sending(shared), "work", level),
            shared,
        )
    left_root = shared[0]
    right_root = shared[1]
    columns = lax.dynamic_slice_in_dim(right_root, place * width, width, 1)
    half = jnp.dot(block, columns, preferred_element_type=jnp.float32).astype(jnp.bfloat16)
    raw = jnp.dot(left_root, half, preferred_element_type=jnp.float32)
    wide = summed.astype(jnp.float32)
    totals = jnp.stack([jnp.sum(raw * raw), jnp.sum(wide * wide)])
    for level in range(2):
        totals = totals + from_partner(totals, "work", level)
    count = block.shape[0] * block.shape[1]
    norm = jnp.sqrt(totals[0] / count + 1e-06)
    graft = jnp.sqrt(totals[1] / count + 1e-06)
    update = (raw * (graft / norm)).astype(jnp.bfloat16)
    return (update, held[None, None])


def solution(mesh):
    placed = (P("dp", None, "work"), P("dp", None, None))
    return jax.shard_map(
        local,
        mesh=mesh,
        in_specs=placed,
        out_specs=(P("dp", "work"), P("dp", "work", None, None, None)),
        check_vma=False,
    )
```

profile of v0, /device:TPU:12, one launch (start us, length us, event | category | flops | bytes accessed | tf_op | source)
XLA Modules:
  0.0 197.8 jit_solution(16025232323559267119)
XLA Ops:
  7.2 0.0 copy-start
  7.2 0.0 reduce-scatter.2.cloned.1.call-start
  7.2 0.7 reduce-scatter.2.cloned.1.call-update
  7.9 80.5 %reduce-scatter.2.cloned.1.call-done = bf16[512,128]{1,0:T(8,128)(2,1)} async-done(((bf16[8192,128]{1,0:T(8,128)(2,1)}), bf16[512,128]{1,0:T(8,128)(2,1)}) %reduce-scatter.2.cloned.1.call-update) | async-done | bytes 131088 | tf_op jit(solution)/shard_map/reduce_scatter | solution.py:45
  88.4 1.9 collective-permute-start
  90.4 1.5 collective-permute-done
  91.9 1.1 maximum_select_fusion.1
  92.9 3.1 %collective-permute-start.1 = (bf16[512,256]{1,0:T(8,128)(2,1)S(1)}, bf16[512,256]{1,0:T(8,128)(2,1)S(1)}, u32[]{:S(2)}, u32[]{:S(2)}) collective-permute-start(bf16[512,256]{1,0:T(8,128)(2,1)S(1)} %maximum_select_fusion.1), channel_id=1, source_target_pairs={{0,2},{1,3},{2,0},{3,1},{4,6},{5,7},{6,4},{7,5},{8,10},{9,11},{10,... | collective-permute-start | bytes 786440 | tf_op jit(solution)/shard_map/ppermute | solution.py:10
  96.1 0.0 copy-done
  96.1 0.1 constant_dynamic-slice_fusion
  96.1 0.1 copy.6
  96.2 0.6 convert_reduce_fusion
  97.5 5.7 %collective-permute-done.1 = bf16[512,256]{1,0:T(8,128)(2,1)S(1)} collective-permute-done((bf16[512,256]{1,0:T(8,128)(2,1)S(1)}, bf16[512,256]{1,0:T(8,128)(2,1)S(1)}, u32[]{:S(2)}, u32[]{:S(2)}) %collective-permute-start.1) | collective-permute-done | bytes 262176 | tf_op jit(solution)/shard_map/ppermute | solution.py:10
  103.2 0.1 maximum_select_fusion
  103.3 35.7 %conditional.1 = (bf16[2,512,512]{2,1,0:T(8,128)(2,1)}, bf16[1,1,2,512,512]{4,3,2,1,0:T(8,128)(2,1)S(1)}) conditional(s32[]{:T(128)} %clamp.3, () %tuple.23, (s32[]{:T(128)}, s32[1,1,2]{2,1,0:T(1,128)S(1)}, pred[2]{0:T(512)(128)(4,1)S(1)}, bf16[512,512]{1,0:T(8,128)(2,1)S(1)}) %tuple.24, ...), branch_computations={%region_2.3_spmd, %region_3.6_spmd, %region_6.9_spmd} | conditional | flops 5393874944 | bytes 56099036 | solution.py:76
  103.5 0.1 iota_compare_fusion.2
  103.6 0.5 convolution_bitcast_fusion
  104.1 0.5 convolution_bitcast_fusion.1
  104.6 0.4 select_reduce_fusion.1
  105.0 1.1 fusion.41
  106.1 0.1 fusion.42
  106.3 0.0 copy-start.1
  106.3 1.0 copy-done.1
  107.2 0.8 multiply_reduce_fusion.1
  108.1 8.2 %convolution_convert_fusion.9 = bf16[2,512,512]{2,1,0:T(8,128)(2,1)} fusion(f32[512,512]{1,0:T(8,128)} %fusion.41, f32[1,512,512]{2,1,0:T(8,128)S(1)} %convolution_bitcast_fusion, f32[1,512,512]{2,1,0:T(8,128)S(1)} %convolution_bitcast_fusion.1, f32[2]{0:T(128)S(1)} %get-tuple-element.29, f32[512,512]{1,0:T(8,128)} %copy-done.1, f32[2]{0:T(128)S(1)} %add_multiply_fusion), kind=kOutput, calls=%fused_computation.57 | convolution fusion | flops 1078460416 | bytes 5242896 | tf_op jit(solution)/shard_map/cond/branch_2_fun/sij,sjk->sik/dot_general | solution.py:18
  116.3 3.8 %fusion.37 = f32[2,512,512]{2,1,0:T(8,128)} fusion(bf16[2,512,512]{2,1,0:T(8,128)(2,1)} %convolution_convert_fusion.9, f32[1,512,512]{2,1,0:T(8,128)S(1)} %convolution_bitcast_fusion, f32[1,512,512]{2,1,0:T(8,128)S(1)} %convolution_bitcast_fusion.1, f32[2]{0:T(128)S(1)} %get-tuple-element.29, f32[512,512]{1,0:T(8,128)} %copy-done.1, f32[2]{0:T(128)S(1)} %add_multiply_fusion), kind=kOutput, calls=%fused_computation.63 | convolution fusion | flops 539492352 | bytes 6291472 | tf_op jit(solution)/shard_map/cond/branch_2_fun/sij,sjk->sik/dot_general | solution.py:18
  120.1 5.1 %convolution_convert_fusion.8 = bf16[2,512,512]{2,1,0:T(8,128)(2,1)} fusion(bf16[512,512]{1,0:T(8,128)(2,1)S(1)} %get-tuple-element.31, f32[512,512]{1,0:T(8,128)} %fusion.41, f32[2,512,512]{2,1,0:T(8,128)} %fusion.37, f32[1,512,512]{2,1,0:T(8,128)S(1)} %convolution_bitcast_fusion, f32[1,512,512]{2,1,0:T(8,128)S(1)} %convolution_bitcast_fusion.1, ...), kind=kOutput, calls=%fused_computation.56 | convolution fusion | flops 1080033280 | bytes 7864336 | tf_op jit(solution)/shard_map/cond/branch_2_fun/sij,sjk->sik/dot_general | solution.py:18
  125.1 8.4 %convolution_convert_fusion.6 = bf16[2,512,512]{2,1,0:T(8,128)(2,1)} fusion(f32[2,512,512]{2,1,0:T(8,128)} %fusion.37, f32[512,512]{1,0:T(8,128)} %fusion.41), kind=kOutput, calls=%fused_computation.54 | convolution fusion | flops 1076363264 | bytes 4194304 | tf_op jit(solution)/shard_map/cond/branch_2_fun/sij,sjk->sik/dot_general | solution.py:18
  133.5 0.0 copy-done.2
  133.5 4.2 %multiply_convert_fusion = bf16[2,512,512]{2,1,0:T(8,128)(2,1)} fusion(bf16[2,512,512]{2,1,0:T(8,128)(2,1)S(1)} %copy-done.5, bf16[2,512,512]{2,1,0:T(8,128)(2,1)} %convolution_convert_fusion.6, f32[2]{0:T(128)S(1)} %get-tuple-element.28, f32[2,512,512]{2,1,0:T(8,128)} %fusion.37, f32[512,512]{1,0:T(8,128)S(1)} %copy-done.2), kind=kOutput, calls=%fused_computation.46 | convolution fusion | flops 1076887552 | bytes 6291464 | tf_op jit(solution)/shard_map/cond/branch_2_fun/sij,sjk->sik/dot_general | solution.py:18
  137.8 1.2 copy.12
  139.0 2.0 %collective-permute-start.2 = (bf16[2,512,512]{2,1,0:T(8,128)(2,1)}, bf16[2,512,512]{2,1,0:T(8,128)(2,1)S(1)}, u32[]{:S(2)}, u32[]{:S(2)}) collective-permute-start(bf16[2,512,512]{2,1,0:T(8,128)(2,1)} %get-tuple-element.22), channel_id=1, source_target_pairs={{0,1},{1,0},{2,3},{3,2},{4,5},{5,4},{6,7},{7,6},{8,9},{9,8},{10,11... | collective-permute-start | bytes 3145736 | tf_op jit(solution)/shard_map/ppermute | solution.py:10
  141.0 2.8 %collective-permute-done.2 = bf16[2,512,512]{2,1,0:T(8,128)(2,1)S(1)} collective-permute-done((bf16[2,512,512]{2,1,0:T(8,128)(2,1)}, bf16[2,512,512]{2,1,0:T(8,128)(2,1)S(1)}, u32[]{:S(2)}, u32[]{:S(2)}) %collective-permute-start.2) | collective-permute-done | bytes 1048608 | tf_op jit(solution)/shard_map/ppermute | solution.py:10
  143.9 1.5 add.78
  145.4 1.9 collective-permute-start.3
  147.3 0.7 multiply_reduce_fusion.2
  148.0 24.5 %collective-permute-done.3 = bf16[2,512,512]{2,1,0:T(8,128)(2,1)} collective-permute-done((bf16[2,512,512]{2,1,0:T(8,128)(2,1)S(1)}, bf16[2,512,512]{2,1,0:T(8,128)(2,1)}, u32[]{:S(2)}, u32[]{:S(2)}) %collective-permute-start.3) | collective-permute-done | bytes 1048608 | tf_op jit(solution)/shard_map/ppermute | solution.py:10
  172.6 1.6 add.79
  174.2 1.3 multiply_reduce_fusion.3
  175.5 1.4 pad_maximum_fusion.1
  176.9 1.9 collective-permute-start.4
  178.8 1.1 collective-permute-done.4
  179.9 1.4 fusion.76
  181.3 2.2 %collective-permute-start.5 = (f32[2]{0:T(128)S(1)}, f32[2]{0:T(128)S(1)}, u32[]{:S(2)}, u32[]{:S(2)}) collective-permute-start(f32[2]{0:T(128)S(1)} %fusion.76), channel_id=1, source_target_pairs={{0,2},{1,3},{2,0},{3,1},{4,6},{5,7},{6,4},{7,5},{8,10},{9,11},{10,... | collective-permute-start | bytes 32 | tf_op jit(solution)/shard_map/ppermute | solution.py:10
  183.5 3.2 %collective-permute-done.5 = f32[2]{0:T(128)S(1)} collective-permute-done((f32[2]{0:T(128)S(1)}, f32[2]{0:T(128)S(1)}, u32[]{:S(2)}, u32[]{:S(2)}) %collective-permute-start.5) | collective-permute-done | bytes 40 | tf_op jit(solution)/shard_map/ppermute | solution.py:10
  186.8 1.4 fusion.77
  188.2 0.7 fusion.59
  190.3 0.7 multiply_convert_fusion.11
  (10 shorter events, 0.1 us)
Async XLA Ops:
  7.2 88.9 %copy-start = (s32[1,8,2]{1,2,0:T(2,128)S(1)}, s32[1,8,2]{1,2,0:T(2,128)}, u32[]{:S(2)}) copy-start(s32[1,8,2]{1,2,0:T(2,128)} %param.6) | copy-start | bytes 196
  7.2 81.3 %reduce-scatter.2.cloned.1.call-start = ((), (), s32[]{:S(2)}) async-start(), calls=%async_computation.1 | async-start | bytes 2228224 | tf_op jit(solution)/shard_map/reduce_scatter | solution.py:45
  88.4 3.4 %collective-permute-start = (bf16[512,128]{1,0:T(8,128)(2,1)}, bf16[512,128]{1,0:T(8,128)(2,1)S(1)}, u32[]{:S(2)}, u32[]{:S(2)}) collective-permute-start(bf16[512,128]{1,0:T(8,128)(2,1)} %reduce-scatter.2.cloned.1.call-done), channel_id=1, source_target_pairs={{0,1},{1,0},{2,3},{3,2},{4,5},{5,4},{6,7},{7,6},{8,9},{9,8},{10,11... | collective-permute-start | bytes 393224 | tf_op jit(solution)/shard_map/ppermute | solution.py:10
  92.9 10.3 %collective-permute-start.1 = (bf16[512,256]{1,0:T(8,128)(2,1)S(1)}, bf16[512,256]{1,0:T(8,128)(2,1)S(1)}, u32[]{:S(2)}, u32[]{:S(2)}) collective-permute-start(bf16[512,256]{1,0:T(8,128)(2,1)S(1)} %maximum_select_fusion.1), channel_id=1, source_target_pairs={{0,2},{1,3},{2,0},{3,1},{4,6},{5,7},{6,4},{7,5},{8,10},{9,11},{10,... | collective-permute-start | bytes 786440 | tf_op jit(solution)/shard_map/ppermute | solution.py:10
  106.3 1.0 copy-start.1
  125.1 8.4 %copy-start.2 = (f32[512,512]{1,0:T(8,128)S(1)}, f32[512,512]{1,0:T(8,128)}, u32[]{:S(2)}) copy-start(f32[512,512]{1,0:T(8,128)} %fusion.41) | copy-start | bytes 3145732 | tf_op jit(solution)/shard_map/cond
  125.1 8.4 %copy-start.5 = (bf16[2,512,512]{2,1,0:T(8,128)(2,1)S(1)}, bf16[2,512,512]{2,1,0:T(8,128)(2,1)}, u32[]{:S(2)}) copy-start(bf16[2,512,512]{2,1,0:T(8,128)(2,1)} %convolution_convert_fusion.8) | copy-start | bytes 3145732 | tf_op jit(solution)/shard_map/cond
  139.0 9.1 %copy-start.3 = (bf16[1,1,2,512,512]{4,3,2,1,0:T(8,128)(2,1)}, bf16[1,1,2,512,512]{4,3,2,1,0:T(8,128)(2,1)S(1)}, u32[]{:S(2)}) copy-start(bf16[1,1,2,512,512]{4,3,2,1,0:T(8,128)(2,1)S(1)} %get-tuple-element.21) | copy-start | bytes 3145732
  139.0 8.3 %copy-start.4 = (bf16[512,128]{1,0:T(8,128)(2,1)S(1)}, bf16[512,128]{1,0:T(8,128)(2,1)}, u32[]{:S(2)}) copy-start(bf16[512,128]{1,0:T(8,128)(2,1)} %reduce-scatter.2.cloned.1.call-done) | copy-start | bytes 393220
  139.0 4.9 %collective-permute-start.2 = (bf16[2,512,512]{2,1,0:T(8,128)(2,1)}, bf16[2,512,512]{2,1,0:T(8,128)(2,1)S(1)}, u32[]{:S(2)}, u32[]{:S(2)}) collective-permute-start(bf16[2,512,512]{2,1,0:T(8,128)(2,1)} %get-tuple-element.22), channel_id=1, source_target_pairs={{0,1},{1,0},{2,3},{3,2},{4,5},{5,4},{6,7},{7,6},{8,9},{9,8},{10,11... | collective-permute-start | bytes 3145736 | tf_op jit(solution)/shard_map/ppermute | solution.py:10
  145.4 27.2 %collective-permute-start.3 = (bf16[2,512,512]{2,1,0:T(8,128)(2,1)S(1)}, bf16[2,512,512]{2,1,0:T(8,128)(2,1)}, u32[]{:S(2)}, u32[]{:S(2)}) collective-permute-start(bf16[2,512,512]{2,1,0:T(8,128)(2,1)S(1)} %add.78), channel_id=1, source_target_pairs={{0,2},{1,3},{2,0},{3,1},{4,6},{5,7},{6,4},{7,5},{8,10},{9,11},{10,... | collective-permute-start | bytes 3145736 | tf_op jit(solution)/shard_map/ppermute | solution.py:10
  176.9 3.0 %collective-permute-start.4 = (f32[2]{0:T(128)S(1)}, f32[2]{0:T(128)S(1)}, u32[]{:S(2)}, u32[]{:S(2)}) collective-permute-start(f32[2]{0:T(128)S(1)} %pad_maximum_fusion.1), channel_id=1, source_target_pairs={{0,1},{1,0},{2,3},{3,2},{4,5},{5,4},{6,7},{7,6},{8,9},{9,8},{10,11... | collective-permute-start | bytes 32 | tf_op jit(solution)/shard_map/ppermute | solution.py:10
  181.3 5.4 %collective-permute-start.5 = (f32[2]{0:T(128)S(1)}, f32[2]{0:T(128)S(1)}, u32[]{:S(2)}, u32[]{:S(2)}) collective-permute-start(f32[2]{0:T(128)S(1)} %fusion.76), channel_id=1, source_target_pairs={{0,2},{1,3},{2,0},{3,1},{4,6},{5,7},{6,4},{7,5},{8,10},{9,11},{10,... | collective-permute-start | bytes 32 | tf_op jit(solution)/shard_map/ppermute | solution.py:10
Sparse Core Ops, SparseCore 0:
  10.8 77.5 reduce-scatter.1
where the time goes:
time: 198 us
  waiting for transfers between devices  120 us (61%)
  matrix products  32 us (16%)
  between operations  16.2 us (8%)
  starting transfers between devices  13.1 us (7%)
  other arithmetic  13.1 us (7%)
  local copies, waits for them, and re-layouts  3.1 us (2%)
    reduce_scatter x1, waiting for transfers between devices, local(): lax.psum_scatter(grads[0].astype(jnp.float32).astype(jnp.bfloat16), 'dp',...  80.5 us
    ppermute x6, waiting for transfers between devices, from_partner(): lax.ppermute(value, axis, [(i, i ^ 1 << distance) for i in range(lax.axis...  38.8 us
    dot_general x5, matrix products, batched(): jnp.einsum('sij,sjk->sik', left, right, preferred_element_type=jnp.float32)  29.7 us
    ppermute x6, starting transfers between devices, from_partner(): lax.ppermute(value, axis, [(i, i ^ 1 << distance) for i in range(lax.axis...  13.1 us
  transfers between devices with their start and end apart: 7, of which 7 were waited for; matrix products, arithmetic and copies ran while one was open for 1% of the time, Pallas kernels for 0%

commit v1 on v0

v1 whole, which is shorter than its diff:
```python
import jax
import jax.numpy as jnp
from jax import lax
from jax.experimental import pallas as pl
from jax.experimental.pallas import tpu as pltpu
from jax.sharding import PartitionSpec as P

ITERS = 3
QUAD = 4


def product(left, right):
    return lax.dot_general(
        left, right, (((1,), (0,)), ((), ())), preferred_element_type=jnp.float32
    )


def gram_matrix(operand, contract):
    return lax.dot_general(
        operand, operand, (((contract,), (contract,)), ((), ())), preferred_element_type=jnp.float32
    )


def total(value):
    return jnp.sum(value, keepdims=True)


def newton_start(stat, diagonal):
    order = stat.shape[0]
    trace = total(jnp.where(diagonal, stat, 0.0))
    damp = 0.1 * (trace / order + 1e-06)
    damped = stat + jnp.where(diagonal, damp, 0.0)
    scale = jnp.sqrt(total(damped * damped) + 1e-06) * 0.25
    return damped * (1.0 / scale), scale


def newton_factor(current, diagonal):
    return ((jnp.where(diagonal, 5.0, 0.0) - current) * 0.25).astype(jnp.bfloat16)


def block_kernel(place_ref, block_ref, update_ref, held_ref, raw_ref):
    block = block_ref[...]
    order = block.shape[0]
    diagonal = lax.broadcasted_iota(jnp.int32, (order, order), 0) == lax.broadcasted_iota(
        jnp.int32, (order, order), 1
    )
    starts = [newton_start(gram_matrix(block, contract), diagonal) for contract in (1, 0)]
    currents = [start[0] for start in starts]
    iterates = [None, None]
    for step in range(ITERS):
        factors = [newton_factor(current, diagonal) for current in currents]
        if step < ITERS - 1:
            squares = [product(f, f).astype(jnp.bfloat16) for f in factors]
            fourths = [product(s, s).astype(jnp.bfloat16) for s in squares]
            currents = [
                product(fourth, current.astype(jnp.bfloat16))
                for fourth, current in zip(fourths, currents)
            ]
        if step == 0:
            iterates = factors
        else:
            iterates = [
                product(iterate.astype(jnp.bfloat16), factor)
                for iterate, factor in zip(iterates, factors)
            ]
    roots = [
        (iterate * lax.rsqrt(jnp.sqrt(start[1]))).astype(jnp.bfloat16)
        for iterate, start in zip(iterates, starts)
    ]
    for slot in range(2):
        held_ref[slot] = jnp.where(place_ref[1 + slot] != 0, roots[slot], jnp.zeros_like(roots[slot]))
    half = product(block, roots[1]).astype(jnp.bfloat16)
    raw = product(roots[0], half)
    raw_ref[...] = raw
    wide = block.astype(jnp.float32)
    count = order * order
    norm = jnp.sqrt(total(raw * raw) / count + 1e-06)
    graft = jnp.sqrt(total(wide * wide) / count + 1e-06)
    width = update_ref.shape[1]
    mine = raw_ref[:, pl.ds(pl.multiple_of(place_ref[0] * width, width), width)]
    update_ref[...] = (mine * (graft / norm)).astype(jnp.bfloat16)


def block_call(place, block, width):
    order = block.shape[0]
    return pl.pallas_call(
        block_kernel,
        out_shape=(
            jax.ShapeDtypeStruct((order, width), jnp.bfloat16),
            jax.ShapeDtypeStruct((2, order, order), jnp.bfloat16),
        ),
        in_specs=[
            pl.BlockSpec(memory_space=pltpu.SMEM),
            pl.BlockSpec(memory_space=pltpu.VMEM),
        ],
        out_specs=(
            pl.BlockSpec(memory_space=pltpu.VMEM),
            pl.BlockSpec(memory_space=pltpu.VMEM),
        ),
        scratch_shapes=[pltpu.VMEM((order, order), jnp.float32)],
        compiler_params=pltpu.CompilerParams(vmem_limit_bytes=48 * 1024 * 1024),
        cost_estimate=pl.CostEstimate(
            flops=40 * order**3, bytes_accessed=8 * order * order, transcendentals=0
        ),
        name="block_roots",
    )(place, block)


def local(grads, worker_list):
    index = lax.axis_index("work")
    place = index % QUAD
    assigned = lax.dynamic_index_in_dim(worker_list[0], index // QUAD, 0, keepdims=False)
    picks = jnp.concatenate([place[None], (assigned == place).astype(jnp.int32)])
    summed = lax.psum_scatter(grads[0], "dp", scatter_dimension=0, tiled=True)
    quads = lax.axis_size("work") // QUAD
    groups = [[QUAD * q + p for p in range(QUAD)] for q in range(quads)]
    block = lax.all_gather(summed, "work", axis=1, tiled=True, axis_index_groups=groups)
    update, held = block_call(picks, block, summed.shape[1])
    return (update, held[None, None])


def solution(mesh):
    placed = (P("dp", None, "work"), P("dp", None, None))
    return jax.shard_map(
        local,
        mesh=mesh,
        in_specs=placed,
        out_specs=(P("dp", "work"), P("dp", "work", None, None, None)),
        check_vma=False,
    )
```

time: 198 us -> 113 us (0.57)
  the two profiles are of different devices: /device:TPU:12 before, /device:TPU:1 now
where the time goes in v1:
time: 113 us
  waiting for transfers between devices  71.5 us (63%)
  blocking collectives  18.3 us (16%)
  between operations  14.1 us (12%)
  Pallas kernels  8.44 us (7%)
    reduce_scatter x1, waiting for transfers between devices, local(): summed = lax.psum_scatter(grads[0], 'dp', scatter_dimension=0, tiled=True)  70.9 us
    all_gather x1, blocking collectives, local(): lax.all_gather(summed, 'work', axis=1, tiled=True, axis_index_groups=groups)  18.3 us
    pallas_call x1, Pallas kernels, block_call(): pl.pallas_call(block_kernel, out_shape=(jax.ShapeDtypeStruct((order, widt...  8.44 us
  transfers between devices with their start and end apart: 1, of which 1 were waited for; matrix products, arithmetic and copies ran while one was open for 0% of the time, Pallas kernels for 0%

profile of v1, /device:TPU:1, one launch (start us, length us, event | category | flops | bytes accessed | tf_op | source)
XLA Modules:
  0.0 112.6 jit_solution(11626657453653067775)
XLA Ops:
  7.2 0.0 copy-start
  7.2 0.0 reduce-scatter.2.cloned.1.call-start
  7.2 0.7 reduce-scatter.2.cloned.1.call-update
  7.9 0.0 copy-done
  7.9 0.2 fusion
  8.1 0.1 pad_add_fusion.place_ref
  8.2 70.9 %reduce-scatter.2.cloned.1.call-done = bf16[512,128]{1,0:T(8,128)(2,1)} async-done(((bf16[8192,128]{1,0:T(8,128)(2,1)}), bf16[512,128]{1,0:T(8,128)(2,1)}) %reduce-scatter.2.cloned.1.call-update) | async-done | bytes 131088 | tf_op jit(solution)/shard_map/reduce_scatter | solution.py:114
  79.1 18.3 %all_gather.3.block_ref = bf16[512,512]{1,0:T(8,128)(2,1)S(1)} all-gather(bf16[512,128]{1,0:T(8,128)(2,1)} %reduce-scatter.2.cloned.1.call-done), channel_id=1, replica_groups={{0,1,2,3},{4,5,6,7},{8,9,10,11},{12,13,14,15},{16,17,18,19},{20,21,22,2..., dimensions={1}, use_global_device_ids=true | all-gather | bytes 655360 | tf_op jit(solution)/shard_map/all_gather | solution.py:117
  97.4 8.4 %block_roots.1 = (bf16[512,128]{1,0:T(8,128)(2,1)}, bf16[2,512,512]{2,1,0:T(8,128)(2,1)}) custom-call(s32[3]{0:T(128)S(1)} %pad_add_fusion.place_ref, bf16[512,512]{1,0:T(8,128)(2,1)S(1)} %all_gather.3.block_ref), custom_call_target="tpu_custom_call" | custom-call | flops 5368709120 | bytes 2097152 | tf_op jit(solution)/shard_map/block_roots/pallas_call | solution.py:86
Async XLA Ops:
  7.2 0.8 copy-start
  7.2 71.9 %reduce-scatter.2.cloned.1.call-start = ((), (), s32[]{:S(2)}) async-start(), calls=%async_computation.1 | async-start | bytes 2228224 | tf_op jit(solution)/shard_map/reduce_scatter | solution.py:114
Sparse Core Ops, SparseCore 0:
  10.8 68.1 reduce-scatter.1

commit v2 on v1

--- a/solution.py
+++ b/solution.py
@@ -1,3 +1,5 @@
+import functools
+
 import jax
 import jax.numpy as jnp
 from jax import lax
@@ -106,12 +108,93 @@
     )(place, block)
 
 
+def add_kernel(parts, parity_ref, *refs):
+    *operands, out_ref = refs
+    rows = out_ref.shape[0]
+    summed = None
+    for operand, (start, only) in zip(operands, parts):
+        value = operand[pl.ds(start, rows), :].astype(jnp.float32)
+        if only is not None:
+            value = jnp.where(parity_ref[0] == only, value, 0.0)
+        summed = value if summed is None else summed + value
+    out_ref[...] = summed.astype(jnp.bfloat16)
+
+
+def add_pieces(parity, rows, name, *terms):
+    arrays = [term[0] for term in terms]
+    width = arrays[0].shape[1]
+    vmem = pl.BlockSpec(memory_space=pltpu.VMEM)
+    return pl.pallas_call(
+        functools.partial(add_kernel, [term[1:] for term in terms]),
+        out_shape=jax.ShapeDtypeStruct((rows, width), jnp.bfloat16),
+        in_specs=[pl.BlockSpec(memory_space=pltpu.SMEM)] + [vmem] * len(arrays),
+        out_specs=vmem,
+        compiler_params=pltpu.CompilerParams(vmem_limit_bytes=16 * 1024 * 1024),
+        cost_estimate=pl.CostEstimate(
+            flops=len(arrays) * rows * width,
+            bytes_accessed=2 * (len(arrays) + 1) * rows * width,
+            transcendentals=0,
+        ),
+        name=name,
+    )(parity, *arrays)
+
+
+def summed_piece(grads):
+    size = lax.axis_size("dp")
+    place = lax.axis_index("dp")
+    pieces = grads.reshape(size, grads.shape[0] // size, grads.shape[1])
+    rows = pieces.shape[1]
+    own = {
+        step: lax.dynamic_index_in_dim(pieces, (place + step) % size, 0, keepdims=False)
+        for step in range(-8, 8)
+    }
+    parity = (place % 2)[None].astype(jnp.int32)
+
+    def shifted(value, step):
+        return lax.ppermute(value, "dp", [(i, (i + step) % size) for i in range(size)])
+
+    def two(first, second):
+        return jnp.concatenate([own[first], own[second]], 0)
+
+    far = {side: shifted(two(7 * side, 5 * side), side) for side in (1, -1)}
+    opposite = lax.ppermute(
+        own[-8], "dp", [(i, (i + (2 if i % 2 == 0 else -2)) % size) for i in range(size)]
+    )
+    near = {side: shifted(two(3 * side, side), side) for side in (1, -1)}
+    six, two_away, four = {}, {}, {}
+    for side, only in ((1, 0), (-1, 1)):
+        joined = add_pieces(
+            parity, rows, "join_six", (far[side], 0, None), (own[6 * side], 0, None), (opposite, 0, only)
+        )
+        six[side] = shifted(joined, 2 * side)
+    for side in (1, -1):
+        joined = add_pieces(parity, rows, "join_two", (near[side], 0, None), (own[2 * side], 0, None))
+        two_away[side] = shifted(joined, 2 * side)
+    for side in (1, -1):
+        joined = add_pieces(
+            parity, rows, "join_four", (far[side], rows, None), (own[4 * side], 0, None), (six[side], 0, None)
+        )
+        four[side] = shifted(joined, 4 * side)
+    return add_pieces(
+        parity,
+        rows,
+        "join_all",
+        (own[0], 0, None),
+        (near[1], rows, None),
+        (near[-1], rows, None),
+        (two_away[1], 0, None),
+        (two_away[-1], 0, None),
+        (four[1], 0, None),
+        (four[-1], 0, None),
+    )
+
+
 def local(grads, worker_list):
     index = lax.axis_index("work")
     place = index % QUAD
     assigned = lax.dynamic_index_in_dim(worker_list[0], index // QUAD, 0, keepdims=False)
     picks = jnp.concatenate([place[None], (assigned == place).astype(jnp.int32)])
-    summed = lax.psum_scatter(grads[0], "dp", scatter_dimension=0, tiled=True)
+    summed = summed_piece(grads[0])
     quads = lax.axis_size("work") // QUAD
     groups = [[QUAD * q + p for p in range(QUAD)] for q in range(quads)]
     block = lax.all_gather(summed, "work", axis=1, tiled=True, axis_index_groups=groups)

time: 113 us -> 82.1 us (0.73)
  waiting for transfers between devices: 71.5 us -> 13.7 us
  starting transfers between devices: 0.04 us -> 47.4 us
  between operations: 14.1 us -> 1.19 us
  blocking collectives: 18.3 us -> 8.11 us
  local copies, waits for them, and re-layouts: 0.01 us -> 2.09 us
    reduce_scatter x1 -> x0, waiting for transfers between devices: 70.9 us -> none  [local(): summed = lax.psum_scatter(grads[0], 'dp', scatter_dimension=0, tiled=True)]
    ppermute x0 -> x11, starting transfers between devices: none -> 47.4 us  [the longest x10 41.7 us: shifted(): lax.ppermute(value, 'dp', [(i, (i + step) % size) for i in range(size)])]
    ppermute x0 -> x11, waiting for transfers between devices: none -> 13.7 us  [the longest x10 13.7 us: shifted(): lax.ppermute(value, 'dp', [(i, (i + step) % size) for i in range(size)])]
    all_gather x1, blocking collectives: 18.3 us -> 8.11 us  [local(): lax.all_gather(summed, 'work', axis=1, tiled=True, axis_index_groups=groups)]
    squeeze x0 -> x1, local copies, waits for them, and re-layouts: none -> 2.08 us  [summed_piece(): lax.dynamic_index_in_dim(pieces, (place + step) % size, 0, keepdims=False)]
  transfers between devices with their start and end apart: 1 -> 11, of which waited for: 1 -> 2; matrix products, arithmetic and copies ran while one was open for 0% -> 0% of each run, Pallas kernels for 0% -> 0%
where the time goes in v2:
time: 82.1 us; the launch traced here: 81.7 us
  starting transfers between devices  47.4 us (58%)
  waiting for transfers between devices  13.7 us (17%)
  Pallas kernels  8.86 us (11%)
  blocking collectives  8.11 us (10%)
  local copies, waits for them, and re-layouts  2.09 us (3%)
  between operations  1.19 us (1%)
    ppermute x10, starting transfers between devices, shifted(): lax.ppermute(value, 'dp', [(i, (i + step) % size) for i in range(size)])  41.7 us
    ppermute x10, waiting for transfers between devices, shifted(): lax.ppermute(value, 'dp', [(i, (i + step) % size) for i in range(size)])  13.7 us
    pallas_call x1, Pallas kernels, block_call(): pl.pallas_call(block_kernel, out_shape=(jax.ShapeDtypeStruct((order, widt...  8.44 us
    all_gather x1, blocking collectives, local(): lax.all_gather(summed, 'work', axis=1, tiled=True, axis_index_groups=groups)  8.11 us
    ppermute x1, starting transfers between devices, summed_piece(): lax.ppermute(own[-8], 'dp', [(i, (i + (2 if i % 2 == 0 else -2)) % size)...  5.73 us
    squeeze x1, local copies, waits for them, and re-layouts, summed_piece(): lax.dynamic_index_in_dim(pieces, (place + step) % size, 0, keepdims=False)  2.08 us
  transfers between devices with their start and end apart: 11, of which 2 were waited for; matrix products, arithmetic and copies ran while one was open for 0% of the time, Pallas kernels for 0%

profile of v2, /device:TPU:1, one launch (start us, length us, event | category | flops | bytes accessed | tf_op | source)
XLA Modules:
  0.0 81.7 jit_solution(4661424372037831856)
XLA Ops:
  0.9 2.1 %dynamic-slice_bitcast_fusion = (bf16[512,128]{1,0:T(8,128)(2,1)S(1)}, bf16[512,128]{1,0:T(8,128)(2,1)S(1)}, bf16[512,128]{1,0:T(8,128)(2,1)S(1)}, bf16[512,128]...) fusion(bf16[16,512,128]{2,1,0:T(8,128)(2,1)} %bitcast.36, ...), kind=kLoop, calls=%fused_computation.4 | loop fusion | bytes 4194368 | tf_op jit(solution)/shard_map/jit(dynamic_index_in_dim)/squeeze | solution.py:148
  3.0 5.7 %collective-permute-start.5 = (bf16[512,128]{1,0:T(8,128)(2,1)S(1)}, bf16[512,128]{1,0:T(8,128)(2,1)S(1)}, u32[]{:S(2)}, u32[]{:S(2)}) collective-permute-start(bf16[512,128]{1,0:T(8,128)(2,1)S(1)} %get-tuple-element.10), channel_id=1, source_target_pairs={{0,64},{32,480},{64,128},{96,32},{128,192},{160,96},{192,256},{224... | collective-permute-start | bytes 393224 | tf_op jit(solution)/shard_map/ppermute | solution.py:160
  8.8 9.3 %collective-permute-start.4 = (bf16[1024,128]{1,0:T(8,128)(2,1)S(1)}, bf16[1024,128]{1,0:T(8,128)(2,1)S(1)}, u32[]{:S(2)}, u32[]{:S(2)}) collective-permute-start(bf16[1024,128]{1,0:T(8,128)(2,1)S(1)} %pad_maximum_fusion.2), channel_id=1, source_target_pairs={{0,32},{32,64},{64,96},{96,128},{128,160},{160,192},{192,224},{224... | collective-permute-start | bytes 786440 | tf_op jit(solution)/shard_map/ppermute | solution.py:154
  18.1 1.9 %collective-permute-start.8 = (bf16[1024,128]{1,0:T(8,128)(2,1)S(1)}, bf16[1024,128]{1,0:T(8,128)(2,1)S(1)}, u32[]{:S(2)}, u32[]{:S(2)}) collective-permute-start(bf16[1024,128]{1,0:T(8,128)(2,1)S(1)} %pad_maximum_fusion.3), channel_id=1, source_target_pairs={{0,480},{32,0},{64,32},{96,64},{128,96},{160,128},{192,160},{224,1... | collective-permute-start | bytes 786440 | tf_op jit(solution)/shard_map/ppermute | solution.py:154
  20.1 3.4 %collective-permute-start = (bf16[1024,128]{1,0:T(8,128)(2,1)S(1)}, bf16[1024,128]{1,0:T(8,128)(2,1)S(1)}, u32[]{:S(2)}, u32[]{:S(2)}) collective-permute-start(bf16[1024,128]{1,0:T(8,128)(2,1)S(1)} %pad_maximum_fusion), channel_id=1, source_target_pairs={{0,32},{32,64},{64,96},{96,128},{128,160},{160,192},{192,224},{224... | collective-permute-start | bytes 786440 | tf_op jit(solution)/shard_map/ppermute | solution.py:154
  23.4 0.0 copy-start
  23.5 3.1 %collective-permute-start.1 = (bf16[1024,128]{1,0:T(8,128)(2,1)S(1)}, bf16[1024,128]{1,0:T(8,128)(2,1)S(1)}, u32[]{:S(2)}, u32[]{:S(2)}) collective-permute-start(bf16[1024,128]{1,0:T(8,128)(2,1)S(1)} %pad_maximum_fusion.1), channel_id=1, source_target_pairs={{0,480},{32,0},{64,32},{96,64},{128,96},{160,128},{192,160},{224,1... | collective-permute-start | bytes 786440 | tf_op jit(solution)/shard_map/ppermute | solution.py:154
  26.6 0.0 collective-permute-done.5.refs_2_
  26.6 0.0 collective-permute-done.4.refs_0_
  26.6 0.1 join_six.2
  26.7 1.9 %collective-permute-start.6 = (bf16[512,128]{1,0:T(8,128)(2,1)S(1)}, bf16[512,128]{1,0:T(8,128)(2,1)S(1)}, u32[]{:S(2)}, u32[]{:S(2)}) collective-permute-start(bf16[512,128]{1,0:T(8,128)(2,1)S(1)} %join_six.2), channel_id=1, source_target_pairs={{0,64},{32,96},{64,128},{96,160},{128,192},{160,224},{192,256},{22... | collective-permute-start | bytes 393224 | tf_op jit(solution)/shard_map/ppermute | solution.py:154
  28.6 0.0 collective-permute-done.8.refs_0_
  28.7 0.1 join_six.3
  28.7 5.5 %collective-permute-start.9 = (bf16[512,128]{1,0:T(8,128)(2,1)S(1)}, bf16[512,128]{1,0:T(8,128)(2,1)S(1)}, u32[]{:S(2)}, u32[]{:S(2)}) collective-permute-start(bf16[512,128]{1,0:T(8,128)(2,1)S(1)} %join_six.3), channel_id=1, source_target_pairs={{0,448},{32,480},{64,0},{96,32},{128,64},{160,96},{192,128},{224,1... | collective-permute-start | bytes 393224 | tf_op jit(solution)/shard_map/ppermute | solution.py:154
  34.2 0.0 collective-permute-done.refs_0_.refs_1_
  34.3 1.9 %collective-permute-start.2 = (bf16[512,128]{1,0:T(8,128)(2,1)S(1)}, bf16[512,128]{1,0:T(8,128)(2,1)S(1)}, u32[]{:S(2)}, u32[]{:S(2)}) collective-permute-start(bf16[512,128]{1,0:T(8,128)(2,1)S(1)} %join_two.2), channel_id=1, source_target_pairs={{0,64},{32,96},{64,128},{96,160},{128,192},{160,224},{192,256},{22... | collective-permute-start | bytes 393224 | tf_op jit(solution)/shard_map/ppermute | solution.py:154
  36.2 0.0 collective-permute-done.1.refs_0_.refs_2_
  36.2 5.5 %collective-permute-start.3 = (bf16[512,128]{1,0:T(8,128)(2,1)S(1)}, bf16[512,128]{1,0:T(8,128)(2,1)S(1)}, u32[]{:S(2)}, u32[]{:S(2)}) collective-permute-start(bf16[512,128]{1,0:T(8,128)(2,1)S(1)} %join_two.3), channel_id=1, source_target_pairs={{0,448},{32,480},{64,0},{96,32},{128,64},{160,96},{192,128},{224,1... | collective-permute-start | bytes 393224 | tf_op jit(solution)/shard_map/ppermute | solution.py:154
  41.7 0.0 collective-permute-done.6.refs_2_
  41.7 0.1 join_four.2
  41.8 4.1 %collective-permute-start.7 = (bf16[512,128]{1,0:T(8,128)(2,1)S(1)}, bf16[512,128]{1,0:T(8,128)(2,1)S(1)}, u32[]{:S(2)}, u32[]{:S(2)}) collective-permute-start(bf16[512,128]{1,0:T(8,128)(2,1)S(1)} %join_four.2), channel_id=1, source_target_pairs={{0,128},{32,160},{64,192},{96,224},{128,256},{160,288},{192,320},{... | collective-permute-start | bytes 393224 | tf_op jit(solution)/shard_map/ppermute | solution.py:154
  45.9 0.0 collective-permute-done.9.refs_2_
  45.9 0.1 join_four.3
  45.9 5.1 %collective-permute-start.10 = (bf16[512,128]{1,0:T(8,128)(2,1)S(1)}, bf16[512,128]{1,0:T(8,128)(2,1)S(1)}, u32[]{:S(2)}, u32[]{:S(2)}) collective-permute-start(bf16[512,128]{1,0:T(8,128)(2,1)S(1)} %join_four.3), channel_id=1, source_target_pairs={{0,384},{32,416},{64,448},{96,480},{128,0},{160,32},{192,64},{224,... | collective-permute-start | bytes 393224 | tf_op jit(solution)/shard_map/ppermute | solution.py:154
  51.1 0.0 copy-done
  51.1 0.2 fusion
  51.3 0.1 pad_add_fusion.place_ref
  51.4 0.0 collective-permute-done.2.refs_3_
  51.4 0.0 collective-permute-done.3.refs_4_
  51.4 7.9 %collective-permute-done.7.refs_5_ = bf16[512,128]{1,0:T(8,128)(2,1)S(1)} collective-permute-done((bf16[512,128]{1,0:T(8,128)(2,1)S(1)}, bf16[512,128]{1,0:T(8,128)(2,1)S(1)}, u32[]{:S(2)}, u32[]{:S(2)}) %collective-permute-start.7) | collective-permute-done | bytes 131104 | tf_op jit(solution)/shard_map/ppermute | solution.py:154
  59.2 5.8 %collective-permute-done.10.refs_6_ = bf16[512,128]{1,0:T(8,128)(2,1)S(1)} collective-permute-done((bf16[512,128]{1,0:T(8,128)(2,1)S(1)}, bf16[512,128]{1,0:T(8,128)(2,1)S(1)}, u32[]{:S(2)}, u32[]{:S(2)}) %collective-permute-start.10) | collective-permute-done | bytes 131104 | tf_op jit(solution)/shard_map/ppermute | solution.py:154
  65.0 0.1 join_all.1
  65.1 8.1 %all_gather.3.block_ref = bf16[512,512]{1,0:T(8,128)(2,1)S(1)} all-gather(bf16[512,128]{1,0:T(8,128)(2,1)S(1)} %join_all.1), channel_id=1, replica_groups={{0,1,2,3},{4,5,6,7},{8,9,10,11},{12,13,14,15},{16,17,18,19},{20,21,22,2..., dimensions={1}, use_global_device_ids=true | all-gather | bytes 655360 | tf_op jit(solution)/shard_map/all_gather | solution.py:200
  73.2 8.4 %block_roots.1 = (bf16[512,128]{1,0:T(8,128)(2,1)}, bf16[2,512,512]{2,1,0:T(8,128)(2,1)}) custom-call(s32[3]{0:T(128)S(1)} %pad_add_fusion.place_ref, bf16[512,512]{1,0:T(8,128)(2,1)S(1)} %all_gather.3.block_ref), custom_call_target="tpu_custom_call" | custom-call | flops 5368709120 | bytes 2097152 | tf_op jit(solution)/shard_map/block_roots/pallas_call | solution.py:88
  (6 shorter events, 0.1 us)
Async XLA Ops:
  3.0 23.6 %collective-permute-start.5 = (bf16[512,128]{1,0:T(8,128)(2,1)S(1)}, bf16[512,128]{1,0:T(8,128)(2,1)S(1)}, u32[]{:S(2)}, u32[]{:S(2)}) collective-permute-start(bf16[512,128]{1,0:T(8,128)(2,1)S(1)} %get-tuple-element.10), channel_id=1, source_target_pairs={{0,64},{32,480},{64,128},{96,32},{128,192},{160,96},{192,256},{224... | collective-permute-start | bytes 393224 | tf_op jit(solution)/shard_map/ppermute | solution.py:160
  8.8 17.9 %collective-permute-start.4 = (bf16[1024,128]{1,0:T(8,128)(2,1)S(1)}, bf16[1024,128]{1,0:T(8,128)(2,1)S(1)}, u32[]{:S(2)}, u32[]{:S(2)}) collective-permute-start(bf16[1024,128]{1,0:T(8,128)(2,1)S(1)} %pad_maximum_fusion.2), channel_id=1, source_target_pairs={{0,32},{32,64},{64,96},{96,128},{128,160},{160,192},{192,224},{224... | collective-permute-start | bytes 786440 | tf_op jit(solution)/shard_map/ppermute | solution.py:154
  18.1 10.5 %collective-permute-start.8 = (bf16[1024,128]{1,0:T(8,128)(2,1)S(1)}, bf16[1024,128]{1,0:T(8,128)(2,1)S(1)}, u32[]{:S(2)}, u32[]{:S(2)}) collective-permute-start(bf16[1024,128]{1,0:T(8,128)(2,1)S(1)} %pad_maximum_fusion.3), channel_id=1, source_target_pairs={{0,480},{32,0},{64,32},{96,64},{128,96},{160,128},{192,160},{224,1... | collective-permute-start | bytes 786440 | tf_op jit(solution)/shard_map/ppermute | solution.py:154
  20.1 14.1 %collective-permute-start = (bf16[1024,128]{1,0:T(8,128)(2,1)S(1)}, bf16[1024,128]{1,0:T(8,128)(2,1)S(1)}, u32[]{:S(2)}, u32[]{:S(2)}) collective-permute-start(bf16[1024,128]{1,0:T(8,128)(2,1)S(1)} %pad_maximum_fusion), channel_id=1, source_target_pairs={{0,32},{32,64},{64,96},{96,128},{128,160},{160,192},{192,224},{224... | collective-permute-start | bytes 786440 | tf_op jit(solution)/shard_map/ppermute | solution.py:154
  23.4 27.7 %copy-start = (s32[1,8,2]{1,2,0:T(2,128)S(1)}, s32[1,8,2]{1,2,0:T(2,128)}, u32[]{:S(2)}) copy-start(s32[1,8,2]{1,2,0:T(2,128)} %param.3) | copy-start | bytes 196
  23.5 12.7 %collective-permute-start.1 = (bf16[1024,128]{1,0:T(8,128)(2,1)S(1)}, bf16[1024,128]{1,0:T(8,128)(2,1)S(1)}, u32[]{:S(2)}, u32[]{:S(2)}) collective-permute-start(bf16[1024,128]{1,0:T(8,128)(2,1)S(1)} %pad_maximum_fusion.1), channel_id=1, source_target_pairs={{0,480},{32,0},{64,32},{96,64},{128,96},{160,128},{192,160},{224,1... | collective-permute-start | bytes 786440 | tf_op jit(solution)/shard_map/ppermute | solution.py:154
  26.7 15.0 %collective-permute-start.6 = (bf16[512,128]{1,0:T(8,128)(2,1)S(1)}, bf16[512,128]{1,0:T(8,128)(2,1)S(1)}, u32[]{:S(2)}, u32[]{:S(2)}) collective-permute-start(bf16[512,128]{1,0:T(8,128)(2,1)S(1)} %join_six.2), channel_id=1, source_target_pairs={{0,64},{32,96},{64,128},{96,160},{128,192},{160,224},{192,256},{22... | collective-permute-start | bytes 393224 | tf_op jit(solution)/shard_map/ppermute | solution.py:154
  28.7 17.1 %collective-permute-start.9 = (bf16[512,128]{1,0:T(8,128)(2,1)S(1)}, bf16[512,128]{1,0:T(8,128)(2,1)S(1)}, u32[]{:S(2)}, u32[]{:S(2)}) collective-permute-start(bf16[512,128]{1,0:T(8,128)(2,1)S(1)} %join_six.3), channel_id=1, source_target_pairs={{0,448},{32,480},{64,0},{96,32},{128,64},{160,96},{192,128},{224,1... | collective-permute-start | bytes 393224 | tf_op jit(solution)/shard_map/ppermute | solution.py:154
  34.3 17.1 %collective-permute-start.2 = (bf16[512,128]{1,0:T(8,128)(2,1)S(1)}, bf16[512,128]{1,0:T(8,128)(2,1)S(1)}, u32[]{:S(2)}, u32[]{:S(2)}) collective-permute-start(bf16[512,128]{1,0:T(8,128)(2,1)S(1)} %join_two.2), channel_id=1, source_target_pairs={{0,64},{32,96},{64,128},{96,160},{128,192},{160,224},{192,256},{22... | collective-permute-start | bytes 393224 | tf_op jit(solution)/shard_map/ppermute | solution.py:154
  36.2 15.1 %collective-permute-start.3 = (bf16[512,128]{1,0:T(8,128)(2,1)S(1)}, bf16[512,128]{1,0:T(8,128)(2,1)S(1)}, u32[]{:S(2)}, u32[]{:S(2)}) collective-permute-start(bf16[512,128]{1,0:T(8,128)(2,1)S(1)} %join_two.3), channel_id=1, source_target_pairs={{0,448},{32,480},{64,0},{96,32},{128,64},{160,96},{192,128},{224,1... | collective-permute-start | bytes 393224 | tf_op jit(solution)/shard_map/ppermute | solution.py:154
  41.8 17.5 %collective-permute-start.7 = (bf16[512,128]{1,0:T(8,128)(2,1)S(1)}, bf16[512,128]{1,0:T(8,128)(2,1)S(1)}, u32[]{:S(2)}, u32[]{:S(2)}) collective-permute-start(bf16[512,128]{1,0:T(8,128)(2,1)S(1)} %join_four.2), channel_id=1, source_target_pairs={{0,128},{32,160},{64,192},{96,224},{128,256},{160,288},{192,320},{... | collective-permute-start | bytes 393224 | tf_op jit(solution)/shard_map/ppermute | solution.py:154
  45.9 19.1 %collective-permute-start.10 = (bf16[512,128]{1,0:T(8,128)(2,1)S(1)}, bf16[512,128]{1,0:T(8,128)(2,1)S(1)}, u32[]{:S(2)}, u32[]{:S(2)}) collective-permute-start(bf16[512,128]{1,0:T(8,128)(2,1)S(1)} %join_four.3), channel_id=1, source_target_pairs={{0,384},{32,416},{64,448},{96,480},{128,0},{160,32},{192,64},{224,... | collective-permute-start | bytes 393224 | tf_op jit(solution)/shard_map/ppermute | solution.py:154

commit v3 on v2

--- a/solution.py
+++ b/solution.py
@@ -7,77 +7,128 @@
 from jax.experimental.pallas import tpu as pltpu
 from jax.sharding import PartitionSpec as P
 
-ITERS = 3
 QUAD = 4
 
 
-def product(left, right):
-    return lax.dot_general(
-        left, right, (((1,), (0,)), ((), ())), preferred_element_type=jnp.float32
-    )
-
-
-def gram_matrix(operand, contract):
-    return lax.dot_general(
-        operand, operand, (((contract,), (contract,)), ((), ())), preferred_element_type=jnp.float32
-    )
+def product(left, right, contract=((1,), (0,))):
+    return lax.dot_general(left, right, (contract, ((), ())), preferred_element_type=jnp.float32)
 
 
 def total(value):
     return jnp.sum(value, keepdims=True)
 
 
-def newton_start(stat, diagonal):
-    order = stat.shape[0]
-    trace = total(jnp.where(diagonal, stat, 0.0))
+def symmetric_product(left, right):
+    half = left.shape[0] // 2
+    return (
+        product(left[:half, :], right[...]),
+        product(left[half:, :], right[:, half:]),
+    )
+
+
+def gram_matrix(block, contract):
+    half = block.shape[0] // 2
+    if contract == 1:
+        first, second = block[:half, :], block[half:, :]
+    else:
+        first, second = block[:, :half], block[:, half:]
+    dims = ((contract,), (contract,))
+    return product(first, block[...], dims), product(second, second, dims)
+
+
+def fill_symmetric(target, upper, corner):
+    half = corner.shape[0]
+    rounded = upper.astype(jnp.bfloat16)
+    target[:half, :] = rounded
+    target[half:, half:] = corner.astype(jnp.bfloat16)
+    target[half:, :half] = rounded[:, half:].T
+
+
+def fill_current_and_factor(current, factor, first, side, second, diagonal):
+    half = first.shape[0]
+    rounded = side.astype(jnp.bfloat16)
+    turned = rounded.T
+    quarter = jnp.bfloat16(-0.25)
+    if current is not None:
+        current[:half, :half] = first.astype(jnp.bfloat16)
+        current[half:, half:] = second.astype(jnp.bfloat16)
+        current[:half, half:] = rounded
+        current[half:, :half] = turned
+    ends = jnp.where(diagonal, 1.25, 0.0)
+    factor[:half, :half] = (ends - first * 0.25).astype(jnp.bfloat16)
+    factor[half:, half:] = (ends - second * 0.25).astype(jnp.bfloat16)
+    factor[:half, half:] = rounded * quarter
+    factor[half:, :half] = turned * quarter
+
+
+def block_kernel(place_ref, block_ref, update_ref, held_ref, raw_ref, work_ref):
+    order = block_ref.shape[0]
+    half = order // 2
+    both = (0, 1)
+    current0, factor0, square, fourth, current1, factor1, iterate, factor2, root = range(9)
+
+    def slot(side, name):
+        return work_ref.at[side, name]
+
+    block = block_ref[...].astype(jnp.float32)
+    trace = total(block * block)
     damp = 0.1 * (trace / order + 1e-06)
-    damped = stat + jnp.where(diagonal, damp, 0.0)
-    scale = jnp.sqrt(total(damped * damped) + 1e-06) * 0.25
-    return damped * (1.0 / scale), scale
-
-
-def newton_factor(current, diagonal):
-    return ((jnp.where(diagonal, 5.0, 0.0) - current) * 0.25).astype(jnp.bfloat16)
-
-
-def block_kernel(place_ref, block_ref, update_ref, held_ref, raw_ref):
-    block = block_ref[...]
-    order = block.shape[0]
-    diagonal = lax.broadcasted_iota(jnp.int32, (order, order), 0) == lax.broadcasted_iota(
-        jnp.int32, (order, order), 1
-    )
-    starts = [newton_start(gram_matrix(block, contract), diagonal) for contract in (1, 0)]
-    currents = [start[0] for start in starts]
-    iterates = [None, None]
-    for step in range(ITERS):
-        factors = [newton_factor(current, diagonal) for current in currents]
-        if step < ITERS - 1:
-            squares = [product(f, f).astype(jnp.bfloat16) for f in factors]
-            fourths = [product(s, s).astype(jnp.bfloat16) for s in squares]
-            currents = [
-                product(fourth, current.astype(jnp.bfloat16))
-                for fourth, current in zip(fourths, currents)
-            ]
-        if step == 0:
-            iterates = factors
-        else:
-            iterates = [
-                product(iterate.astype(jnp.bfloat16), factor)
-                for iterate, factor in zip(iterates, factors)
-            ]
-    roots = [
-        (iterate * lax.rsqrt(jnp.sqrt(start[1]))).astype(jnp.bfloat16)
-        for iterate, start in zip(iterates, starts)
-    ]
-    for slot in range(2):
-        held_ref[slot] = jnp.where(place_ref[1 + slot] != 0, roots[slot], jnp.zeros_like(roots[slot]))
-    half = product(block, roots[1]).astype(jnp.bfloat16)
-    raw = product(roots[0], half)
+    diagonal = lax.broadcasted_iota(jnp.int32, (half, half), 0) == lax.broadcasted_iota(
+        jnp.int32, (half, half), 1
+    )
+    stats = [gram_matrix(block_ref, contract) for contract in (1, 0)]
+    upper, corner = stats[0]
+    first, side = upper[:, :half], upper[:, half:]
+    squares = total(first * first) + 2.0 * total(side * side) + total(corner * corner)
+    scale = jnp.sqrt(squares + damp * (2.0 * trace + order * damp) + 1e-06) * 0.25
+    inverse = 1.0 / scale
+    shift = jnp.where(diagonal, damp * inverse, 0.0)
+    for k in both:
+        upper, corner = stats[k]
+        fill_current_and_factor(
+            slot(k, current0),
+            slot(k, factor0),
+            upper[:, :half] * inverse + shift,
+            upper[:, half:] * inverse,
+            corner * inverse + shift,
+            diagonal,
+        )
+    for now, factor, after, factor_after in (
+        (current0, factor0, current1, factor1),
+        (current1, factor1, None, factor2),
+    ):
+        for k in both:
+            fill_symmetric(slot(k, square), *symmetric_product(slot(k, factor), slot(k, factor)))
+        for k in both:
+            fill_symmetric(slot(k, fourth), *symmetric_product(slot(k, square), slot(k, square)))
+        if factor == factor1:
+            for k in both:
+                fill_symmetric(
+                    slot(k, iterate), *symmetric_product(slot(k, factor0), slot(k, factor1))
+                )
+        for k in both:
+            upper, corner = symmetric_product(slot(k, fourth), slot(k, now))
+            fill_current_and_factor(
+                None if after is None else slot(k, after),
+                slot(k, factor_after),
+                upper[:, :half],
+                upper[:, half:],
+                corner,
+                diagonal,
+            )
+    power = lax.rsqrt(jnp.sqrt(scale))
+    for k in (1, 0):
+        upper, corner = symmetric_product(slot(k, iterate), slot(k, factor2))
+        fill_symmetric(slot(k, root), upper * power, corner * power)
+    for k in both:
+        made = work_ref[k, root]
+        held_ref[k] = jnp.where(place_ref[1 + k] != 0, made, jnp.zeros_like(made))
+    half_done = product(block_ref[...], work_ref[1, root]).astype(jnp.bfloat16)
+    raw = product(work_ref[0, root], half_done)
     raw_ref[...] = raw
-    wide = block.astype(jnp.float32)
     count = order * order
     norm = jnp.sqrt(total(raw * raw) / count + 1e-06)
-    graft = jnp.sqrt(total(wide * wide) / count + 1e-06)
+    graft = jnp.sqrt(trace / count + 1e-06)
     width = update_ref.shape[1]
     mine = raw_ref[:, pl.ds(pl.multiple_of(place_ref[0] * width, width), width)]
     update_ref[...] = (mine * (graft / norm)).astype(jnp.bfloat16)
@@ -99,10 +150,13 @@
             pl.BlockSpec(memory_space=pltpu.VMEM),
             pl.BlockSpec(memory_space=pltpu.VMEM),
         ),
-        scratch_shapes=[pltpu.VMEM((order, order), jnp.float32)],
+        scratch_shapes=[
+            pltpu.VMEM((order, order), jnp.float32),
+            pltpu.VMEM((2, 9, order, order), jnp.bfloat16),
+        ],
         compiler_params=pltpu.CompilerParams(vmem_limit_bytes=48 * 1024 * 1024),
         cost_estimate=pl.CostEstimate(
-            flops=40 * order**3, bytes_accessed=8 * order * order, transcendentals=0
+            flops=31 * order**3, bytes_accessed=8 * order * order, transcendentals=0
         ),
         name="block_roots",
     )(place, block)
@@ -156,21 +210,21 @@
     def two(first, second):
         return jnp.concatenate([own[first], own[second]], 0)
 
-    far = {side: shifted(two(7 * side, 5 * side), side) for side in (1, -1)}
+    far = {side: shifted(two(7 * side, 5 * side), side) for side in (-1, 1)}
     opposite = lax.ppermute(
         own[-8], "dp", [(i, (i + (2 if i % 2 == 0 else -2)) % size) for i in range(size)]
     )
-    near = {side: shifted(two(3 * side, side), side) for side in (1, -1)}
+    near = {side: shifted(two(3 * side, side), side) for side in (-1, 1)}
     six, two_away, four = {}, {}, {}
-    for side, only in ((1, 0), (-1, 1)):
+    for side, only in ((-1, 1), (1, 0)):
         joined = add_pieces(
             parity, rows, "join_six", (far[side], 0, None), (own[6 * side], 0, None), (opposite, 0, only)
         )
         six[side] = shifted(joined, 2 * side)
-    for side in (1, -1):
+    for side in (-1, 1):
         joined = add_pieces(parity, rows, "join_two", (near[side], 0, None), (own[2 * side], 0, None))
         two_away[side] = shifted(joined, 2 * side)
-    for side in (1, -1):
+    for side in (-1, 1):
         joined = add_pieces(
             parity, rows, "join_four", (far[side], rows, None), (own[4 * side], 0, None), (six[side], 0, None)
         )

time: 82.1 us -> 80.1 us (0.976)
  Pallas kernels: 8.86 us -> 6.84 us
    pallas_call x1, Pallas kernels: 8.44 us -> 6.42 us  [block_call(): pl.pallas_call(block_kernel, out_shape=(jax.ShapeDtypeStruct((order, widt...]
where the time goes in v3:
time: 80.1 us; the launch traced here: 79.7 us
  starting transfers between devices  47.4 us (59%)
  waiting for transfers between devices  13.7 us (17%)
  blocking collectives  8.11 us (10%)
  Pallas kernels  6.84 us (9%)
  local copies, waits for them, and re-layouts  2.09 us (3%)
  between operations  1.19 us (1%)
    ppermute x10, starting transfers between devices, shifted(): lax.ppermute(value, 'dp', [(i, (i + step) % size) for i in range(size)])  41.7 us
    ppermute x10, waiting for transfers between devices, shifted(): lax.ppermute(value, 'dp', [(i, (i + step) % size) for i in range(size)])  13.7 us
    all_gather x1, blocking collectives, local(): lax.all_gather(summed, 'work', axis=1, tiled=True, axis_index_groups=groups)  8.11 us
    pallas_call x1, Pallas kernels, block_call(): pl.pallas_call(block_kernel, out_shape=(jax.ShapeDtypeStruct((order, widt...  6.42 us
    ppermute x1, starting transfers between devices, summed_piece(): lax.ppermute(own[-8], 'dp', [(i, (i + (2 if i % 2 == 0 else -2)) % size)...  5.73 us
    squeeze x1, local copies, waits for them, and re-layouts, summed_piece(): lax.dynamic_index_in_dim(pieces, (place + step) % size, 0, keepdims=False)  2.08 us
  transfers between devices with their start and end apart: 11, of which 2 were waited for; matrix products, arithmetic and copies ran while one was open for 0% of the time, Pallas kernels for 0%

profile of v3, /device:TPU:1, one launch (start us, length us, event | category | flops | bytes accessed | tf_op | source)
XLA Modules:
  0.0 79.7 jit_solution(17927861939139351659)
XLA Ops:
  0.9 2.1 %dynamic-slice_bitcast_fusion = (bf16[512,128]{1,0:T(8,128)(2,1)S(1)}, bf16[512,128]{1,0:T(8,128)(2,1)S(1)}, bf16[512,128]{1,0:T(8,128)(2,1)S(1)}, bf16[512,128]...) fusion(bf16[16,512,128]{2,1,0:T(8,128)(2,1)} %bitcast.36, ...), kind=kLoop, calls=%fused_computation.4 | loop fusion | bytes 4194368 | tf_op jit(solution)/shard_map/jit(dynamic_index_in_dim)/squeeze | solution.py:202
  3.0 5.7 %collective-permute-start.5 = (bf16[512,128]{1,0:T(8,128)(2,1)S(1)}, bf16[512,128]{1,0:T(8,128)(2,1)S(1)}, u32[]{:S(2)}, u32[]{:S(2)}) collective-permute-start(bf16[512,128]{1,0:T(8,128)(2,1)S(1)} %get-tuple-element.10), channel_id=1, source_target_pairs={{0,64},{32,480},{64,128},{96,32},{128,192},{160,96},{192,256},{224... | collective-permute-start | bytes 393224 | tf_op jit(solution)/shard_map/ppermute | solution.py:214
  8.8 9.3 %collective-permute-start.4 = (bf16[1024,128]{1,0:T(8,128)(2,1)S(1)}, bf16[1024,128]{1,0:T(8,128)(2,1)S(1)}, u32[]{:S(2)}, u32[]{:S(2)}) collective-permute-start(bf16[1024,128]{1,0:T(8,128)(2,1)S(1)} %pad_maximum_fusion.2), channel_id=1, source_target_pairs={{0,32},{32,64},{64,96},{96,128},{128,160},{160,192},{192,224},{224... | collective-permute-start | bytes 786440 | tf_op jit(solution)/shard_map/ppermute | solution.py:208
  18.1 1.9 %collective-permute-start.8 = (bf16[1024,128]{1,0:T(8,128)(2,1)S(1)}, bf16[1024,128]{1,0:T(8,128)(2,1)S(1)}, u32[]{:S(2)}, u32[]{:S(2)}) collective-permute-start(bf16[1024,128]{1,0:T(8,128)(2,1)S(1)} %pad_maximum_fusion.3), channel_id=1, source_target_pairs={{0,480},{32,0},{64,32},{96,64},{128,96},{160,128},{192,160},{224,1... | collective-permute-start | bytes 786440 | tf_op jit(solution)/shard_map/ppermute | solution.py:208
  20.1 3.4 %collective-permute-start = (bf16[1024,128]{1,0:T(8,128)(2,1)S(1)}, bf16[1024,128]{1,0:T(8,128)(2,1)S(1)}, u32[]{:S(2)}, u32[]{:S(2)}) collective-permute-start(bf16[1024,128]{1,0:T(8,128)(2,1)S(1)} %pad_maximum_fusion), channel_id=1, source_target_pairs={{0,32},{32,64},{64,96},{96,128},{128,160},{160,192},{192,224},{224... | collective-permute-start | bytes 786440 | tf_op jit(solution)/shard_map/ppermute | solution.py:208
  23.4 0.0 copy-start
  23.5 3.1 %collective-permute-start.1 = (bf16[1024,128]{1,0:T(8,128)(2,1)S(1)}, bf16[1024,128]{1,0:T(8,128)(2,1)S(1)}, u32[]{:S(2)}, u32[]{:S(2)}) collective-permute-start(bf16[1024,128]{1,0:T(8,128)(2,1)S(1)} %pad_maximum_fusion.1), channel_id=1, source_target_pairs={{0,480},{32,0},{64,32},{96,64},{128,96},{160,128},{192,160},{224,1... | collective-permute-start | bytes 786440 | tf_op jit(solution)/shard_map/ppermute | solution.py:208
  26.6 0.0 collective-permute-done.5.refs_2_
  26.6 0.0 collective-permute-done.4.refs_0_
  26.6 0.1 join_six.2
  26.7 1.9 %collective-permute-start.6 = (bf16[512,128]{1,0:T(8,128)(2,1)S(1)}, bf16[512,128]{1,0:T(8,128)(2,1)S(1)}, u32[]{:S(2)}, u32[]{:S(2)}) collective-permute-start(bf16[512,128]{1,0:T(8,128)(2,1)S(1)} %join_six.2), channel_id=1, source_target_pairs={{0,64},{32,96},{64,128},{96,160},{128,192},{160,224},{192,256},{22... | collective-permute-start | bytes 393224 | tf_op jit(solution)/shard_map/ppermute | solution.py:208
  28.6 0.0 collective-permute-done.8.refs_0_
  28.7 0.1 join_six.3
  28.7 5.5 %collective-permute-start.9 = (bf16[512,128]{1,0:T(8,128)(2,1)S(1)}, bf16[512,128]{1,0:T(8,128)(2,1)S(1)}, u32[]{:S(2)}, u32[]{:S(2)}) collective-permute-start(bf16[512,128]{1,0:T(8,128)(2,1)S(1)} %join_six.3), channel_id=1, source_target_pairs={{0,448},{32,480},{64,0},{96,32},{128,64},{160,96},{192,128},{224,1... | collective-permute-start | bytes 393224 | tf_op jit(solution)/shard_map/ppermute | solution.py:208
  34.2 0.0 collective-permute-done.refs_0_.refs_1_
  34.3 1.9 %collective-permute-start.2 = (bf16[512,128]{1,0:T(8,128)(2,1)S(1)}, bf16[512,128]{1,0:T(8,128)(2,1)S(1)}, u32[]{:S(2)}, u32[]{:S(2)}) collective-permute-start(bf16[512,128]{1,0:T(8,128)(2,1)S(1)} %join_two.2), channel_id=1, source_target_pairs={{0,64},{32,96},{64,128},{96,160},{128,192},{160,224},{192,256},{22... | collective-permute-start | bytes 393224 | tf_op jit(solution)/shard_map/ppermute | solution.py:208
  36.2 0.0 collective-permute-done.1.refs_0_.refs_2_
  36.2 5.5 %collective-permute-start.3 = (bf16[512,128]{1,0:T(8,128)(2,1)S(1)}, bf16[512,128]{1,0:T(8,128)(2,1)S(1)}, u32[]{:S(2)}, u32[]{:S(2)}) collective-permute-start(bf16[512,128]{1,0:T(8,128)(2,1)S(1)} %join_two.3), channel_id=1, source_target_pairs={{0,448},{32,480},{64,0},{96,32},{128,64},{160,96},{192,128},{224,1... | collective-permute-start | bytes 393224 | tf_op jit(solution)/shard_map/ppermute | solution.py:208
  41.7 0.0 collective-permute-done.6.refs_2_
  41.7 0.1 join_four.2
  41.8 4.1 %collective-permute-start.7 = (bf16[512,128]{1,0:T(8,128)(2,1)S(1)}, bf16[512,128]{1,0:T(8,128)(2,1)S(1)}, u32[]{:S(2)}, u32[]{:S(2)}) collective-permute-start(bf16[512,128]{1,0:T(8,128)(2,1)S(1)} %join_four.2), channel_id=1, source_target_pairs={{0,128},{32,160},{64,192},{96,224},{128,256},{160,288},{192,320},{... | collective-permute-start | bytes 393224 | tf_op jit(solution)/shard_map/ppermute | solution.py:208
  45.9 0.0 collective-permute-done.9.refs_2_
  45.9 0.1 join_four.3
  45.9 5.1 %collective-permute-start.10 = (bf16[512,128]{1,0:T(8,128)(2,1)S(1)}, bf16[512,128]{1,0:T(8,128)(2,1)S(1)}, u32[]{:S(2)}, u32[]{:S(2)}) collective-permute-start(bf16[512,128]{1,0:T(8,128)(2,1)S(1)} %join_four.3), channel_id=1, source_target_pairs={{0,384},{32,416},{64,448},{96,480},{128,0},{160,32},{192,64},{224,... | collective-permute-start | bytes 393224 | tf_op jit(solution)/shard_map/ppermute | solution.py:208
  51.1 0.0 copy-done
  51.1 0.2 fusion
  51.3 0.1 pad_add_fusion.place_ref
  51.4 0.0 collective-permute-done.2.refs_3_
  51.4 0.0 collective-permute-done.3.refs_4_
  51.4 7.9 %collective-permute-done.7.refs_5_ = bf16[512,128]{1,0:T(8,128)(2,1)S(1)} collective-permute-done((bf16[512,128]{1,0:T(8,128)(2,1)S(1)}, bf16[512,128]{1,0:T(8,128)(2,1)S(1)}, u32[]{:S(2)}, u32[]{:S(2)}) %collective-permute-start.7) | collective-permute-done | bytes 131104 | tf_op jit(solution)/shard_map/ppermute | solution.py:208
  59.2 5.8 %collective-permute-done.10.refs_6_ = bf16[512,128]{1,0:T(8,128)(2,1)S(1)} collective-permute-done((bf16[512,128]{1,0:T(8,128)(2,1)S(1)}, bf16[512,128]{1,0:T(8,128)(2,1)S(1)}, u32[]{:S(2)}, u32[]{:S(2)}) %collective-permute-start.10) | collective-permute-done | bytes 131104 | tf_op jit(solution)/shard_map/ppermute | solution.py:208
  65.0 0.1 join_all.1
  65.1 8.1 %all_gather.3.block_ref = bf16[512,512]{1,0:T(8,128)(2,1)S(1)} all-gather(bf16[512,128]{1,0:T(8,128)(2,1)S(1)} %join_all.1), channel_id=1, replica_groups={{0,1,2,3},{4,5,6,7},{8,9,10,11},{12,13,14,15},{16,17,18,19},{20,21,22,2..., dimensions={1}, use_global_device_ids=true | all-gather | bytes 655360 | tf_op jit(solution)/shard_map/all_gather | solution.py:254
  73.2 6.4 %block_roots.1 = (bf16[512,128]{1,0:T(8,128)(2,1)}, bf16[2,512,512]{2,1,0:T(8,128)(2,1)}) custom-call(s32[3]{0:T(128)S(1)} %pad_add_fusion.place_ref, bf16[512,512]{1,0:T(8,128)(2,1)S(1)} %all_gather.3.block_ref), custom_call_target="tpu_custom_call" | custom-call | flops 4160749568 | bytes 2097152 | tf_op jit(solution)/shard_map/block_roots/pallas_call | solution.py:139
  (6 shorter events, 0.1 us)
Async XLA Ops:
  3.0 23.6 %collective-permute-start.5 = (bf16[512,128]{1,0:T(8,128)(2,1)S(1)}, bf16[512,128]{1,0:T(8,128)(2,1)S(1)}, u32[]{:S(2)}, u32[]{:S(2)}) collective-permute-start(bf16[512,128]{1,0:T(8,128)(2,1)S(1)} %get-tuple-element.10), channel_id=1, source_target_pairs={{0,64},{32,480},{64,128},{96,32},{128,192},{160,96},{192,256},{224... | collective-permute-start | bytes 393224 | tf_op jit(solution)/shard_map/ppermute | solution.py:214
  8.8 17.9 %collective-permute-start.4 = (bf16[1024,128]{1,0:T(8,128)(2,1)S(1)}, bf16[1024,128]{1,0:T(8,128)(2,1)S(1)}, u32[]{:S(2)}, u32[]{:S(2)}) collective-permute-start(bf16[1024,128]{1,0:T(8,128)(2,1)S(1)} %pad_maximum_fusion.2), channel_id=1, source_target_pairs={{0,32},{32,64},{64,96},{96,128},{128,160},{160,192},{192,224},{224... | collective-permute-start | bytes 786440 | tf_op jit(solution)/shard_map/ppermute | solution.py:208
  18.1 10.5 %collective-permute-start.8 = (bf16[1024,128]{1,0:T(8,128)(2,1)S(1)}, bf16[1024,128]{1,0:T(8,128)(2,1)S(1)}, u32[]{:S(2)}, u32[]{:S(2)}) collective-permute-start(bf16[1024,128]{1,0:T(8,128)(2,1)S(1)} %pad_maximum_fusion.3), channel_id=1, source_target_pairs={{0,480},{32,0},{64,32},{96,64},{128,96},{160,128},{192,160},{224,1... | collective-permute-start | bytes 786440 | tf_op jit(solution)/shard_map/ppermute | solution.py:208
  20.1 14.1 %collective-permute-start = (bf16[1024,128]{1,0:T(8,128)(2,1)S(1)}, bf16[1024,128]{1,0:T(8,128)(2,1)S(1)}, u32[]{:S(2)}, u32[]{:S(2)}) collective-permute-start(bf16[1024,128]{1,0:T(8,128)(2,1)S(1)} %pad_maximum_fusion), channel_id=1, source_target_pairs={{0,32},{32,64},{64,96},{96,128},{128,160},{160,192},{192,224},{224... | collective-permute-start | bytes 786440 | tf_op jit(solution)/shard_map/ppermute | solution.py:208
  23.4 27.7 %copy-start = (s32[1,8,2]{1,2,0:T(2,128)S(1)}, s32[1,8,2]{1,2,0:T(2,128)}, u32[]{:S(2)}) copy-start(s32[1,8,2]{1,2,0:T(2,128)} %param.3) | copy-start | bytes 196
  23.5 12.7 %collective-permute-start.1 = (bf16[1024,128]{1,0:T(8,128)(2,1)S(1)}, bf16[1024,128]{1,0:T(8,128)(2,1)S(1)}, u32[]{:S(2)}, u32[]{:S(2)}) collective-permute-start(bf16[1024,128]{1,0:T(8,128)(2,1)S(1)} %pad_maximum_fusion.1), channel_id=1, source_target_pairs={{0,480},{32,0},{64,32},{96,64},{128,96},{160,128},{192,160},{224,1... | collective-permute-start | bytes 786440 | tf_op jit(solution)/shard_map/ppermute | solution.py:208
  26.7 15.0 %collective-permute-start.6 = (bf16[512,128]{1,0:T(8,128)(2,1)S(1)}, bf16[512,128]{1,0:T(8,128)(2,1)S(1)}, u32[]{:S(2)}, u32[]{:S(2)}) collective-permute-start(bf16[512,128]{1,0:T(8,128)(2,1)S(1)} %join_six.2), channel_id=1, source_target_pairs={{0,64},{32,96},{64,128},{96,160},{128,192},{160,224},{192,256},{22... | collective-permute-start | bytes 393224 | tf_op jit(solution)/shard_map/ppermute | solution.py:208
  28.7 17.1 %collective-permute-start.9 = (bf16[512,128]{1,0:T(8,128)(2,1)S(1)}, bf16[512,128]{1,0:T(8,128)(2,1)S(1)}, u32[]{:S(2)}, u32[]{:S(2)}) collective-permute-start(bf16[512,128]{1,0:T(8,128)(2,1)S(1)} %join_six.3), channel_id=1, source_target_pairs={{0,448},{32,480},{64,0},{96,32},{128,64},{160,96},{192,128},{224,1... | collective-permute-start | bytes 393224 | tf_op jit(solution)/shard_map/ppermute | solution.py:208
  34.3 17.1 %collective-permute-start.2 = (bf16[512,128]{1,0:T(8,128)(2,1)S(1)}, bf16[512,128]{1,0:T(8,128)(2,1)S(1)}, u32[]{:S(2)}, u32[]{:S(2)}) collective-permute-start(bf16[512,128]{1,0:T(8,128)(2,1)S(1)} %join_two.2), channel_id=1, source_target_pairs={{0,64},{32,96},{64,128},{96,160},{128,192},{160,224},{192,256},{22... | collective-permute-start | bytes 393224 | tf_op jit(solution)/shard_map/ppermute | solution.py:208
  36.2 15.1 %collective-permute-start.3 = (bf16[512,128]{1,0:T(8,128)(2,1)S(1)}, bf16[512,128]{1,0:T(8,128)(2,1)S(1)}, u32[]{:S(2)}, u32[]{:S(2)}) collective-permute-start(bf16[512,128]{1,0:T(8,128)(2,1)S(1)} %join_two.3), channel_id=1, source_target_pairs={{0,448},{32,480},{64,0},{96,32},{128,64},{160,96},{192,128},{224,1... | collective-permute-start | bytes 393224 | tf_op jit(solution)/shard_map/ppermute | solution.py:208
  41.8 17.5 %collective-permute-start.7 = (bf16[512,128]{1,0:T(8,128)(2,1)S(1)}, bf16[512,128]{1,0:T(8,128)(2,1)S(1)}, u32[]{:S(2)}, u32[]{:S(2)}) collective-permute-start(bf16[512,128]{1,0:T(8,128)(2,1)S(1)} %join_four.2), channel_id=1, source_target_pairs={{0,128},{32,160},{64,192},{96,224},{128,256},{160,288},{192,320},{... | collective-permute-start | bytes 393224 | tf_op jit(solution)/shard_map/ppermute | solution.py:208
  45.9 19.1 %collective-permute-start.10 = (bf16[512,128]{1,0:T(8,128)(2,1)S(1)}, bf16[512,128]{1,0:T(8,128)(2,1)S(1)}, u32[]{:S(2)}, u32[]{:S(2)}) collective-permute-start(bf16[512,128]{1,0:T(8,128)(2,1)S(1)} %join_four.3), channel_id=1, source_target_pairs={{0,384},{32,416},{64,448},{96,480},{128,0},{160,32},{192,64},{224,... | collective-permute-start | bytes 393224 | tf_op jit(solution)/shard_map/ppermute | solution.py:208

commit v4 on v3

--- a/solution.py
+++ b/solution.py
@@ -210,21 +210,21 @@
     def two(first, second):
         return jnp.concatenate([own[first], own[second]], 0)
 
-    far = {side: shifted(two(7 * side, 5 * side), side) for side in (-1, 1)}
+    far = {side: shifted(two(7 * side, 5 * side), side) for side in (1, -1)}
     opposite = lax.ppermute(
         own[-8], "dp", [(i, (i + (2 if i % 2 == 0 else -2)) % size) for i in range(size)]
     )
-    near = {side: shifted(two(3 * side, side), side) for side in (-1, 1)}
+    near = {side: shifted(two(3 * side, side), side) for side in (1, -1)}
     six, two_away, four = {}, {}, {}
-    for side, only in ((-1, 1), (1, 0)):
+    for side, only in ((1, 0), (-1, 1)):
         joined = add_pieces(
             parity, rows, "join_six", (far[side], 0, None), (own[6 * side], 0, None), (opposite, 0, only)
         )
         six[side] = shifted(joined, 2 * side)
-    for side in (-1, 1):
+    for side in (1, -1):
         joined = add_pieces(parity, rows, "join_two", (near[side], 0, None), (own[2 * side], 0, None))
         two_away[side] = shifted(joined, 2 * side)
-    for side in (-1, 1):
+    for side in (1, -1):
         joined = add_pieces(
             parity, rows, "join_four", (far[side], rows, None), (own[4 * side], 0, None), (six[side], 0, None)
         )
@@ -234,8 +234,8 @@
         rows,
         "join_all",
         (own[0], 0, None),
+        (near[-1], rows, None),
         (near[1], rows, None),
-        (near[-1], rows, None),
         (two_away[1], 0, None),
         (two_away[-1], 0, None),
         (four[1], 0, None),

time: 80.1 us -> 76.9 us (0.960)
  the two profiles are of different devices: /device:TPU:1 before, /device:TPU:89 now
where the time goes in v4:
time: 76.9 us; the launch traced here: 76.5 us
  starting transfers between devices  42.4 us (55%)
  blocking collectives  16.4 us (21%)
  waiting for transfers between devices  7.25 us (9%)
  Pallas kernels  6.85 us (9%)
  local copies, waits for them, and re-layouts  2.09 us (3%)
  between operations  1.19 us (2%)
    ppermute x10, starting transfers between devices, shifted(): lax.ppermute(value, 'dp', [(i, (i + step) % size) for i in range(size)])  36.3 us
    all_gather x1, blocking collectives, local(): lax.all_gather(summed, 'work', axis=1, tiled=True, axis_index_groups=groups)  16.4 us
    ppermute x10, waiting for transfers between devices, shifted(): lax.ppermute(value, 'dp', [(i, (i + step) % size) for i in range(size)])  7.24 us
    pallas_call x1, Pallas kernels, block_call(): pl.pallas_call(block_kernel, out_shape=(jax.ShapeDtypeStruct((order, widt...  6.43 us
    ppermute x1, starting transfers between devices, summed_piece(): lax.ppermute(own[-8], 'dp', [(i, (i + (2 if i % 2 == 0 else -2)) % size)...  6.11 us
    squeeze x1, local copies, waits for them, and re-layouts, summed_piece(): lax.dynamic_index_in_dim(pieces, (place + step) % size, 0, keepdims=False)  2.08 us
  transfers between devices with their start and end apart: 11, of which 2 were waited for; matrix products, arithmetic and copies ran while one was open for 0% of the time, Pallas kernels for 0%

profile of v4, /device:TPU:89, one launch (start us, length us, event | category | flops | bytes accessed | tf_op | source)
XLA Modules:
  0.0 76.5 jit_solution(8591680083019065155)
XLA Ops:
  0.9 2.1 %dynamic-slice_bitcast_fusion = (bf16[512,128]{1,0:T(8,128)(2,1)S(1)}, bf16[512,128]{1,0:T(8,128)(2,1)S(1)}, bf16[512,128]{1,0:T(8,128)(2,1)S(1)}, bf16[512,128]...) fusion(bf16[16,512,128]{2,1,0:T(8,128)(2,1)} %bitcast.36, ...), kind=kLoop, calls=%fused_computation.4 | loop fusion | bytes 4194368 | tf_op jit(solution)/shard_map/jit(dynamic_index_in_dim)/squeeze | solution.py:202
  3.0 6.1 %collective-permute-start.5 = (bf16[512,128]{1,0:T(8,128)(2,1)S(1)}, bf16[512,128]{1,0:T(8,128)(2,1)S(1)}, u32[]{:S(2)}, u32[]{:S(2)}) collective-permute-start(bf16[512,128]{1,0:T(8,128)(2,1)S(1)} %get-tuple-element.10), channel_id=1, source_target_pairs={{0,64},{32,480},{64,128},{96,32},{128,192},{160,96},{192,256},{224... | collective-permute-start | bytes 393224 | tf_op jit(solution)/shard_map/ppermute | solution.py:214
  9.1 1.9 %collective-permute-start.4 = (bf16[1024,128]{1,0:T(8,128)(2,1)S(1)}, bf16[1024,128]{1,0:T(8,128)(2,1)S(1)}, u32[]{:S(2)}, u32[]{:S(2)}) collective-permute-start(bf16[1024,128]{1,0:T(8,128)(2,1)S(1)} %pad_maximum_fusion.2), channel_id=1, source_target_pairs={{0,32},{32,64},{64,96},{96,128},{128,160},{160,192},{192,224},{224... | collective-permute-start | bytes 786440 | tf_op jit(solution)/shard_map/ppermute | solution.py:208
  11.1 6.3 %collective-permute-start.8 = (bf16[1024,128]{1,0:T(8,128)(2,1)S(1)}, bf16[1024,128]{1,0:T(8,128)(2,1)S(1)}, u32[]{:S(2)}, u32[]{:S(2)}) collective-permute-start(bf16[1024,128]{1,0:T(8,128)(2,1)S(1)} %pad_maximum_fusion.3), channel_id=1, source_target_pairs={{0,480},{32,0},{64,32},{96,64},{128,96},{160,128},{192,160},{224,1... | collective-permute-start | bytes 786440 | tf_op jit(solution)/shard_map/ppermute | solution.py:208
  17.4 3.4 %collective-permute-start = (bf16[1024,128]{1,0:T(8,128)(2,1)S(1)}, bf16[1024,128]{1,0:T(8,128)(2,1)S(1)}, u32[]{:S(2)}, u32[]{:S(2)}) collective-permute-start(bf16[1024,128]{1,0:T(8,128)(2,1)S(1)} %pad_maximum_fusion), channel_id=1, source_target_pairs={{0,480},{32,0},{64,32},{96,64},{128,96},{160,128},{192,160},{224,1... | collective-permute-start | bytes 786440 | tf_op jit(solution)/shard_map/ppermute | solution.py:208
  20.8 0.0 copy-start
  20.8 1.9 %collective-permute-start.1 = (bf16[1024,128]{1,0:T(8,128)(2,1)S(1)}, bf16[1024,128]{1,0:T(8,128)(2,1)S(1)}, u32[]{:S(2)}, u32[]{:S(2)}) collective-permute-start(bf16[1024,128]{1,0:T(8,128)(2,1)S(1)} %pad_maximum_fusion.1), channel_id=1, source_target_pairs={{0,32},{32,64},{64,96},{96,128},{128,160},{160,192},{192,224},{224... | collective-permute-start | bytes 786440 | tf_op jit(solution)/shard_map/ppermute | solution.py:208
  22.8 0.0 collective-permute-done.5.refs_2_
  22.8 0.0 collective-permute-done.4.refs_0_
  22.8 0.1 join_six.2
  22.9 3.5 %collective-permute-start.6 = (bf16[512,128]{1,0:T(8,128)(2,1)S(1)}, bf16[512,128]{1,0:T(8,128)(2,1)S(1)}, u32[]{:S(2)}, u32[]{:S(2)}) collective-permute-start(bf16[512,128]{1,0:T(8,128)(2,1)S(1)} %join_six.2), channel_id=1, source_target_pairs={{0,64},{32,96},{64,128},{96,160},{128,192},{160,224},{192,256},{22... | collective-permute-start | bytes 393224 | tf_op jit(solution)/shard_map/ppermute | solution.py:208
  26.4 0.0 collective-permute-done.8.refs_0_
  26.4 0.1 join_six.3
  26.5 2.6 %collective-permute-start.9 = (bf16[512,128]{1,0:T(8,128)(2,1)S(1)}, bf16[512,128]{1,0:T(8,128)(2,1)S(1)}, u32[]{:S(2)}, u32[]{:S(2)}) collective-permute-start(bf16[512,128]{1,0:T(8,128)(2,1)S(1)} %join_six.3), channel_id=1, source_target_pairs={{0,448},{32,480},{64,0},{96,32},{128,64},{160,96},{192,128},{224,1... | collective-permute-start | bytes 393224 | tf_op jit(solution)/shard_map/ppermute | solution.py:208
  29.1 0.0 collective-permute-done.refs_0_.refs_1_
  29.2 4.3 %collective-permute-start.3 = (bf16[512,128]{1,0:T(8,128)(2,1)S(1)}, bf16[512,128]{1,0:T(8,128)(2,1)S(1)}, u32[]{:S(2)}, u32[]{:S(2)}) collective-permute-start(bf16[512,128]{1,0:T(8,128)(2,1)S(1)} %join_two.3), channel_id=1, source_target_pairs={{0,448},{32,480},{64,0},{96,32},{128,64},{160,96},{192,128},{224,1... | collective-permute-start | bytes 393224 | tf_op jit(solution)/shard_map/ppermute | solution.py:208
  33.5 0.0 collective-permute-done.1.refs_0_.refs_2_
  33.6 3.1 %collective-permute-start.2 = (bf16[512,128]{1,0:T(8,128)(2,1)S(1)}, bf16[512,128]{1,0:T(8,128)(2,1)S(1)}, u32[]{:S(2)}, u32[]{:S(2)}) collective-permute-start(bf16[512,128]{1,0:T(8,128)(2,1)S(1)} %join_two.2), channel_id=1, source_target_pairs={{0,64},{32,96},{64,128},{96,160},{128,192},{160,224},{192,256},{22... | collective-permute-start | bytes 393224 | tf_op jit(solution)/shard_map/ppermute | solution.py:208
  36.7 0.0 collective-permute-done.6.refs_2_
  36.7 0.1 join_four.2
  36.7 5.9 %collective-permute-start.7 = (bf16[512,128]{1,0:T(8,128)(2,1)S(1)}, bf16[512,128]{1,0:T(8,128)(2,1)S(1)}, u32[]{:S(2)}, u32[]{:S(2)}) collective-permute-start(bf16[512,128]{1,0:T(8,128)(2,1)S(1)} %join_four.2), channel_id=1, source_target_pairs={{0,128},{32,160},{64,192},{96,224},{128,256},{160,288},{192,320},{... | collective-permute-start | bytes 393224 | tf_op jit(solution)/shard_map/ppermute | solution.py:208
  42.7 0.0 collective-permute-done.9.refs_2_
  42.7 0.1 join_four.3
  42.7 3.3 %collective-permute-start.10 = (bf16[512,128]{1,0:T(8,128)(2,1)S(1)}, bf16[512,128]{1,0:T(8,128)(2,1)S(1)}, u32[]{:S(2)}, u32[]{:S(2)}) collective-permute-start(bf16[512,128]{1,0:T(8,128)(2,1)S(1)} %join_four.3), channel_id=1, source_target_pairs={{0,384},{32,416},{64,448},{96,480},{128,0},{160,32},{192,64},{224,... | collective-permute-start | bytes 393224 | tf_op jit(solution)/shard_map/ppermute | solution.py:208
  46.0 0.0 copy-done
  46.0 0.2 fusion
  46.2 0.1 pad_add_fusion.place_ref
  46.3 0.0 collective-permute-done.3.refs_4_
  46.3 0.0 collective-permute-done.2.refs_3_
  46.3 6.5 %collective-permute-done.7.refs_5_ = bf16[512,128]{1,0:T(8,128)(2,1)S(1)} collective-permute-done((bf16[512,128]{1,0:T(8,128)(2,1)S(1)}, bf16[512,128]{1,0:T(8,128)(2,1)S(1)}, u32[]{:S(2)}, u32[]{:S(2)}) %collective-permute-start.7) | collective-permute-done | bytes 131104 | tf_op jit(solution)/shard_map/ppermute | solution.py:208
  52.8 0.8 collective-permute-done.10.refs_6_
  53.5 0.1 join_all.1
  53.7 16.4 %all_gather.3.block_ref = bf16[512,512]{1,0:T(8,128)(2,1)S(1)} all-gather(bf16[512,128]{1,0:T(8,128)(2,1)S(1)} %join_all.1), channel_id=1, replica_groups={{0,1,2,3},{4,5,6,7},{8,9,10,11},{12,13,14,15},{16,17,18,19},{20,21,22,2..., dimensions={1}, use_global_device_ids=true | all-gather | bytes 655360 | tf_op jit(solution)/shard_map/all_gather | solution.py:254
  70.1 6.4 %block_roots.1 = (bf16[512,128]{1,0:T(8,128)(2,1)}, bf16[2,512,512]{2,1,0:T(8,128)(2,1)}) custom-call(s32[3]{0:T(128)S(1)} %pad_add_fusion.place_ref, bf16[512,512]{1,0:T(8,128)(2,1)S(1)} %all_gather.3.block_ref), custom_call_target="tpu_custom_call" | custom-call | flops 4160749568 | bytes 2097152 | tf_op jit(solution)/shard_map/block_roots/pallas_call | solution.py:139
  (6 shorter events, 0.1 us)
Async XLA Ops:
  3.0 19.8 %collective-permute-start.5 = (bf16[512,128]{1,0:T(8,128)(2,1)S(1)}, bf16[512,128]{1,0:T(8,128)(2,1)S(1)}, u32[]{:S(2)}, u32[]{:S(2)}) collective-permute-start(bf16[512,128]{1,0:T(8,128)(2,1)S(1)} %get-tuple-element.10), channel_id=1, source_target_pairs={{0,64},{32,480},{64,128},{96,32},{128,192},{160,96},{192,256},{224... | collective-permute-start | bytes 393224 | tf_op jit(solution)/shard_map/ppermute | solution.py:214
  9.1 13.6 %collective-permute-start.4 = (bf16[1024,128]{1,0:T(8,128)(2,1)S(1)}, bf16[1024,128]{1,0:T(8,128)(2,1)S(1)}, u32[]{:S(2)}, u32[]{:S(2)}) collective-permute-start(bf16[1024,128]{1,0:T(8,128)(2,1)S(1)} %pad_maximum_fusion.2), channel_id=1, source_target_pairs={{0,32},{32,64},{64,96},{96,128},{128,160},{160,192},{192,224},{224... | collective-permute-start | bytes 786440 | tf_op jit(solution)/shard_map/ppermute | solution.py:208
  11.1 15.3 %collective-permute-start.8 = (bf16[1024,128]{1,0:T(8,128)(2,1)S(1)}, bf16[1024,128]{1,0:T(8,128)(2,1)S(1)}, u32[]{:S(2)}, u32[]{:S(2)}) collective-permute-start(bf16[1024,128]{1,0:T(8,128)(2,1)S(1)} %pad_maximum_fusion.3), channel_id=1, source_target_pairs={{0,480},{32,0},{64,32},{96,64},{128,96},{160,128},{192,160},{224,1... | collective-permute-start | bytes 786440 | tf_op jit(solution)/shard_map/ppermute | solution.py:208
  17.4 11.7 %collective-permute-start = (bf16[1024,128]{1,0:T(8,128)(2,1)S(1)}, bf16[1024,128]{1,0:T(8,128)(2,1)S(1)}, u32[]{:S(2)}, u32[]{:S(2)}) collective-permute-start(bf16[1024,128]{1,0:T(8,128)(2,1)S(1)} %pad_maximum_fusion), channel_id=1, source_target_pairs={{0,480},{32,0},{64,32},{96,64},{128,96},{160,128},{192,160},{224,1... | collective-permute-start | bytes 786440 | tf_op jit(solution)/shard_map/ppermute | solution.py:208
  20.8 25.2 %copy-start = (s32[1,8,2]{1,2,0:T(2,128)S(1)}, s32[1,8,2]{1,2,0:T(2,128)}, u32[]{:S(2)}) copy-start(s32[1,8,2]{1,2,0:T(2,128)} %param.3) | copy-start | bytes 196
  20.8 12.7 %collective-permute-start.1 = (bf16[1024,128]{1,0:T(8,128)(2,1)S(1)}, bf16[1024,128]{1,0:T(8,128)(2,1)S(1)}, u32[]{:S(2)}, u32[]{:S(2)}) collective-permute-start(bf16[1024,128]{1,0:T(8,128)(2,1)S(1)} %pad_maximum_fusion.1), channel_id=1, source_target_pairs={{0,32},{32,64},{64,96},{96,128},{128,160},{160,192},{192,224},{224... | collective-permute-start | bytes 786440 | tf_op jit(solution)/shard_map/ppermute | solution.py:208
  22.9 13.8 %collective-permute-start.6 = (bf16[512,128]{1,0:T(8,128)(2,1)S(1)}, bf16[512,128]{1,0:T(8,128)(2,1)S(1)}, u32[]{:S(2)}, u32[]{:S(2)}) collective-permute-start(bf16[512,128]{1,0:T(8,128)(2,1)S(1)} %join_six.2), channel_id=1, source_target_pairs={{0,64},{32,96},{64,128},{96,160},{128,192},{160,224},{192,256},{22... | collective-permute-start | bytes 393224 | tf_op jit(solution)/shard_map/ppermute | solution.py:208
  26.5 16.2 %collective-permute-start.9 = (bf16[512,128]{1,0:T(8,128)(2,1)S(1)}, bf16[512,128]{1,0:T(8,128)(2,1)S(1)}, u32[]{:S(2)}, u32[]{:S(2)}) collective-permute-start(bf16[512,128]{1,0:T(8,128)(2,1)S(1)} %join_six.3), channel_id=1, source_target_pairs={{0,448},{32,480},{64,0},{96,32},{128,64},{160,96},{192,128},{224,1... | collective-permute-start | bytes 393224 | tf_op jit(solution)/shard_map/ppermute | solution.py:208
  29.2 17.1 %collective-permute-start.3 = (bf16[512,128]{1,0:T(8,128)(2,1)S(1)}, bf16[512,128]{1,0:T(8,128)(2,1)S(1)}, u32[]{:S(2)}, u32[]{:S(2)}) collective-permute-start(bf16[512,128]{1,0:T(8,128)(2,1)S(1)} %join_two.3), channel_id=1, source_target_pairs={{0,448},{32,480},{64,0},{96,32},{128,64},{160,96},{192,128},{224,1... | collective-permute-start | bytes 393224 | tf_op jit(solution)/shard_map/ppermute | solution.py:208
  33.6 12.8 %collective-permute-start.2 = (bf16[512,128]{1,0:T(8,128)(2,1)S(1)}, bf16[512,128]{1,0:T(8,128)(2,1)S(1)}, u32[]{:S(2)}, u32[]{:S(2)}) collective-permute-start(bf16[512,128]{1,0:T(8,128)(2,1)S(1)} %join_two.2), channel_id=1, source_target_pairs={{0,64},{32,96},{64,128},{96,160},{128,192},{160,224},{192,256},{22... | collective-permute-start | bytes 393224 | tf_op jit(solution)/shard_map/ppermute | solution.py:208
  36.7 16.0 %collective-permute-start.7 = (bf16[512,128]{1,0:T(8,128)(2,1)S(1)}, bf16[512,128]{1,0:T(8,128)(2,1)S(1)}, u32[]{:S(2)}, u32[]{:S(2)}) collective-permute-start(bf16[512,128]{1,0:T(8,128)(2,1)S(1)} %join_four.2), channel_id=1, source_target_pairs={{0,128},{32,160},{64,192},{96,224},{128,256},{160,288},{192,320},{... | collective-permute-start | bytes 393224 | tf_op jit(solution)/shard_map/ppermute | solution.py:208
  42.7 10.8 %collective-permute-start.10 = (bf16[512,128]{1,0:T(8,128)(2,1)S(1)}, bf16[512,128]{1,0:T(8,128)(2,1)S(1)}, u32[]{:S(2)}, u32[]{:S(2)}) collective-permute-start(bf16[512,128]{1,0:T(8,128)(2,1)S(1)} %join_four.3), channel_id=1, source_target_pairs={{0,384},{32,416},{64,448},{96,480},{128,0},{160,32},{192,64},{224,... | collective-permute-start | bytes 393224 | tf_op jit(solution)/shard_map/ppermute | solution.py:208

commit v5 on v4

--- a/solution.py
+++ b/solution.py
@@ -162,24 +162,40 @@
     )(place, block)
 
 
-def add_kernel(parts, parity_ref, *refs):
+OPPOSITE = "opposite"
+ROUTE = (
+    (1, (7, 5)),
+    (-1, (-7, -5)),
+    OPPOSITE,
+    (-1, (-3, -1)),
+    (1, (3, 1)),
+    (2, (6,)),
+    (-2, (-6,)),
+    (-2, (-4,)),
+    (2, (4,)),
+    (2, (2,)),
+    (-2, (-2,)),
+)
+
+
+def join_kernel(sums, parity_ref, *refs):
     *operands, out_ref = refs
     rows = out_ref.shape[0]
     summed = None
-    for operand, (start, only) in zip(operands, parts):
-        value = operand[pl.ds(start, rows), :].astype(jnp.float32)
+    for operand, start, only in sums:
+        value = operands[operand][pl.ds(start, rows), :].astype(jnp.float32)
         if only is not None:
             value = jnp.where(parity_ref[0] == only, value, 0.0)
         summed = value if summed is None else summed + value
     out_ref[...] = summed.astype(jnp.bfloat16)
 
 
-def add_pieces(parity, rows, name, *terms):
+def join(parity, rows, name, terms):
     arrays = [term[0] for term in terms]
     width = arrays[0].shape[1]
     vmem = pl.BlockSpec(memory_space=pltpu.VMEM)
     return pl.pallas_call(
-        functools.partial(add_kernel, [term[1:] for term in terms]),
+        functools.partial(join_kernel, [(k, *term[1:]) for k, term in enumerate(terms)]),
         out_shape=jax.ShapeDtypeStruct((rows, width), jnp.bfloat16),
         in_specs=[pl.BlockSpec(memory_space=pltpu.SMEM)] + [vmem] * len(arrays),
         out_specs=vmem,
@@ -198,49 +214,33 @@
     place = lax.axis_index("dp")
     pieces = grads.reshape(size, grads.shape[0] // size, grads.shape[1])
     rows = pieces.shape[1]
-    own = {
-        step: lax.dynamic_index_in_dim(pieces, (place + step) % size, 0, keepdims=False)
-        for step in range(-8, 8)
-    }
     parity = (place % 2)[None].astype(jnp.int32)
 
-    def shifted(value, step):
-        return lax.ppermute(value, "dp", [(i, (i + step) % size) for i in range(size)])
-
-    def two(first, second):
-        return jnp.concatenate([own[first], own[second]], 0)
-
-    far = {side: shifted(two(7 * side, 5 * side), side) for side in (1, -1)}
-    opposite = lax.ppermute(
-        own[-8], "dp", [(i, (i + (2 if i % 2 == 0 else -2)) % size) for i in range(size)]
-    )
-    near = {side: shifted(two(3 * side, side), side) for side in (1, -1)}
-    six, two_away, four = {}, {}, {}
-    for side, only in ((1, 0), (-1, 1)):
-        joined = add_pieces(
-            parity, rows, "join_six", (far[side], 0, None), (own[6 * side], 0, None), (opposite, 0, only)
-        )
-        six[side] = shifted(joined, 2 * side)
-    for side in (1, -1):
-        joined = add_pieces(parity, rows, "join_two", (near[side], 0, None), (own[2 * side], 0, None))
-        two_away[side] = shifted(joined, 2 * side)
-    for side in (1, -1):
-        joined = add_pieces(
-            parity, rows, "join_four", (far[side], rows, None), (own[4 * side], 0, None), (six[side], 0, None)
-        )
-        four[side] = shifted(joined, 4 * side)
-    return add_pieces(
-        parity,
-        rows,
-        "join_all",
-        (own[0], 0, None),
-        (near[-1], rows, None),
-        (near[1], rows, None),
-        (two_away[1], 0, None),
-        (two_away[-1], 0, None),
-        (four[1], 0, None),
-        (four[-1], 0, None),
-    )
+    def own(distance):
+        return lax.dynamic_index_in_dim(pieces, (place + distance) % size, 0, keepdims=False)
+
+    def moved(value, shift):
+        return lax.ppermute(value, "dp", [(i, (i + shift(i)) % size) for i in range(size)])
+
+    terms = {distance: [(own(distance), 0, None)] for distance in range(-7, 8)}
+    for step in ROUTE:
+        if step == OPPOSITE:
+            arrived = moved(own(-8), lambda i: 2 if i % 2 == 0 else -2)
+            terms[6].append((arrived, 0, 0))
+            terms[-6].append((arrived, 0, 1))
+            continue
+        shift, distances = step
+        leaving = [terms.pop(distance) for distance in distances]
+        if all(len(parts) == 1 for parts in leaving):
+            value = jnp.concatenate([parts[0][0] for parts in leaving], 0)
+        else:
+            (parts,) = leaving
+            value = join(parity, rows, "join_pieces", parts)
+        arrived = moved(value, lambda i, shift=shift: shift)
+        for order, distance in enumerate(distances):
+            terms[distance - shift].append((arrived, order * rows, None))
+    (parts,) = terms.values()
+    return join(parity, rows, "join_all", parts)
 
 
 def local(grads, worker_list):

time: 76.9 us -> 76.2 us (level)
  the two profiles are of different devices: /device:TPU:89 before, /device:TPU:1 now
where the time goes in v5:
time: 76.2 us; the launch traced here: 75.7 us
  starting transfers between devices  43.1 us (57%)
  blocking collectives  13.6 us (18%)
  waiting for transfers between devices  8.63 us (11%)
  Pallas kernels  6.85 us (9%)
  local copies, waits for them, and re-layouts  2.08 us (3%)
  between operations  1.16 us (2%)
    ppermute x11, starting transfers between devices, moved(): lax.ppermute(value, 'dp', [(i, (i + shift(i)) % size) for i in range(size)])  43.1 us
    all_gather x1, blocking collectives, local(): lax.all_gather(summed, 'work', axis=1, tiled=True, axis_index_groups=groups)  13.6 us
    ppermute x11, waiting for transfers between devices, moved(): lax.ppermute(value, 'dp', [(i, (i + shift(i)) % size) for i in range(size)])  8.63 us
    pallas_call x1, Pallas kernels, block_call(): pl.pallas_call(block_kernel, out_shape=(jax.ShapeDtypeStruct((order, widt...  6.43 us
    squeeze x1, local copies, waits for them, and re-layouts, own(): lax.dynamic_index_in_dim(pieces, (place + distance) % size, 0, keepdims=F...  2.08 us
  transfers between devices with their start and end apart: 11, of which 4 were waited for; matrix products, arithmetic and copies ran while one was open for 0% of the time, Pallas kernels for 0%

profile of v5, /device:TPU:1, one launch (start us, length us, event | category | flops | bytes accessed | tf_op | source)
XLA Modules:
  0.0 75.7 jit_solution(13217467219279935877)
XLA Ops:
  0.9 2.1 %dynamic-slice_bitcast_fusion = (bf16[512,128]{1,0:T(8,128)(2,1)S(1)}, bf16[512,128]{1,0:T(8,128)(2,1)S(1)}, bf16[512,128]{1,0:T(8,128)(2,1)S(1)}, bf16[512,128]...) fusion(bf16[16,512,128]{2,1,0:T(8,128)(2,1)} %bitcast.36, ...), kind=kLoop, calls=%fused_computation.4 | loop fusion | bytes 4194368 | tf_op jit(solution)/shard_map/jit(dynamic_index_in_dim)/squeeze | solution.py:220
  3.0 4.4 %collective-permute-start.2 = (bf16[1024,128]{1,0:T(8,128)(2,1)S(1)}, bf16[1024,128]{1,0:T(8,128)(2,1)S(1)}, u32[]{:S(2)}, u32[]{:S(2)}) collective-permute-start(bf16[1024,128]{1,0:T(8,128)(2,1)S(1)} %pad_maximum_fusion.2), channel_id=1, source_target_pairs={{0,32},{32,64},{64,96},{96,128},{128,160},{160,192},{192,224},{224... | collective-permute-start | bytes 786440 | tf_op jit(solution)/shard_map/ppermute | solution.py:223
  7.4 9.5 %collective-permute-start.7 = (bf16[1024,128]{1,0:T(8,128)(2,1)S(1)}, bf16[1024,128]{1,0:T(8,128)(2,1)S(1)}, u32[]{:S(2)}, u32[]{:S(2)}) collective-permute-start(bf16[1024,128]{1,0:T(8,128)(2,1)S(1)} %pad_maximum_fusion.3), channel_id=1, source_target_pairs={{0,480},{32,0},{64,32},{96,64},{128,96},{160,128},{192,160},{224,1... | collective-permute-start | bytes 786440 | tf_op jit(solution)/shard_map/ppermute | solution.py:223
  16.9 1.9 %collective-permute-start.3 = (bf16[512,128]{1,0:T(8,128)(2,1)S(1)}, bf16[512,128]{1,0:T(8,128)(2,1)S(1)}, u32[]{:S(2)}, u32[]{:S(2)}) collective-permute-start(bf16[512,128]{1,0:T(8,128)(2,1)S(1)} %get-tuple-element.11), channel_id=1, source_target_pairs={{0,64},{32,480},{64,128},{96,32},{128,192},{160,96},{192,256},{224... | collective-permute-start | bytes 393224 | tf_op jit(solution)/shard_map/ppermute | solution.py:223
  18.9 4.5 %collective-permute-start.1 = (bf16[1024,128]{1,0:T(8,128)(2,1)S(1)}, bf16[1024,128]{1,0:T(8,128)(2,1)S(1)}, u32[]{:S(2)}, u32[]{:S(2)}) collective-permute-start(bf16[1024,128]{1,0:T(8,128)(2,1)S(1)} %pad_maximum_fusion.1), channel_id=1, source_target_pairs={{0,32},{32,64},{64,96},{96,128},{128,160},{160,192},{192,224},{224... | collective-permute-start | bytes 786440 | tf_op jit(solution)/shard_map/ppermute | solution.py:223
  23.5 1.3 %collective-permute-done.3.refs_2_ = bf16[512,128]{1,0:T(8,128)(2,1)S(1)} collective-permute-done((bf16[512,128]{1,0:T(8,128)(2,1)S(1)}, bf16[512,128]{1,0:T(8,128)(2,1)S(1)}, u32[]{:S(2)}, u32[]{:S(2)}) %collective-permute-start.3) | collective-permute-done | bytes 131104 | tf_op jit(solution)/shard_map/ppermute | solution.py:223
  24.8 0.0 collective-permute-done.2.refs_1_
  24.8 0.0 copy-start
  24.8 0.1 join_pieces.6
  24.9 1.9 %collective-permute-start.4 = (bf16[512,128]{1,0:T(8,128)(2,1)S(1)}, bf16[512,128]{1,0:T(8,128)(2,1)S(1)}, u32[]{:S(2)}, u32[]{:S(2)}) collective-permute-start(bf16[512,128]{1,0:T(8,128)(2,1)S(1)} %join_pieces.6), channel_id=1, source_target_pairs={{0,64},{32,96},{64,128},{96,160},{128,192},{160,224},{192,256},{22... | collective-permute-start | bytes 393224 | tf_op jit(solution)/shard_map/ppermute | solution.py:223
  26.8 0.0 collective-permute-done.7.refs_1_
  26.8 0.1 join_pieces.9
  26.9 5.5 %collective-permute-start.8 = (bf16[512,128]{1,0:T(8,128)(2,1)S(1)}, bf16[512,128]{1,0:T(8,128)(2,1)S(1)}, u32[]{:S(2)}, u32[]{:S(2)}) collective-permute-start(bf16[512,128]{1,0:T(8,128)(2,1)S(1)} %join_pieces.9), channel_id=1, source_target_pairs={{0,448},{32,480},{64,0},{96,32},{128,64},{160,96},{192,128},{224,1... | collective-permute-start | bytes 393224 | tf_op jit(solution)/shard_map/ppermute | solution.py:223
  32.4 2.2 %collective-permute-start = (bf16[1024,128]{1,0:T(8,128)(2,1)S(1)}, bf16[1024,128]{1,0:T(8,128)(2,1)S(1)}, u32[]{:S(2)}, u32[]{:S(2)}) collective-permute-start(bf16[1024,128]{1,0:T(8,128)(2,1)S(1)} %pad_maximum_fusion), channel_id=1, source_target_pairs={{0,480},{32,0},{64,32},{96,64},{128,96},{160,128},{192,160},{224,1... | collective-permute-start | bytes 786440 | tf_op jit(solution)/shard_map/ppermute | solution.py:223
  34.6 0.0 collective-permute-done.4.refs_2_
  34.6 0.1 join_pieces.7
  34.7 1.9 %collective-permute-start.5 = (bf16[512,128]{1,0:T(8,128)(2,1)S(1)}, bf16[512,128]{1,0:T(8,128)(2,1)S(1)}, u32[]{:S(2)}, u32[]{:S(2)}) collective-permute-start(bf16[512,128]{1,0:T(8,128)(2,1)S(1)} %join_pieces.7), channel_id=1, source_target_pairs={{0,64},{32,96},{64,128},{96,160},{128,192},{160,224},{192,256},{22... | collective-permute-start | bytes 393224 | tf_op jit(solution)/shard_map/ppermute | solution.py:223
  36.6 0.7 collective-permute-done.8.refs_2_
  37.3 0.1 join_pieces.10
  37.4 6.4 %collective-permute-start.9 = (bf16[512,128]{1,0:T(8,128)(2,1)S(1)}, bf16[512,128]{1,0:T(8,128)(2,1)S(1)}, u32[]{:S(2)}, u32[]{:S(2)}) collective-permute-start(bf16[512,128]{1,0:T(8,128)(2,1)S(1)} %join_pieces.10), channel_id=1, source_target_pairs={{0,448},{32,480},{64,0},{96,32},{128,64},{160,96},{192,128},{224,1... | collective-permute-start | bytes 393224 | tf_op jit(solution)/shard_map/ppermute | solution.py:223
  43.8 0.0 collective-permute-done.1.refs_1_.refs_2_
  43.8 0.0 collective-permute-done.5.refs_2_
  43.8 0.1 join_pieces.8
  43.8 1.9 %collective-permute-start.6 = (bf16[512,128]{1,0:T(8,128)(2,1)S(1)}, bf16[512,128]{1,0:T(8,128)(2,1)S(1)}, u32[]{:S(2)}, u32[]{:S(2)}) collective-permute-start(bf16[512,128]{1,0:T(8,128)(2,1)S(1)} %join_pieces.8), channel_id=1, source_target_pairs={{0,64},{32,96},{64,128},{96,160},{128,192},{160,224},{192,256},{22... | collective-permute-start | bytes 393224 | tf_op jit(solution)/shard_map/ppermute | solution.py:223
  45.8 0.0 collective-permute-done.refs_1_
  45.8 2.9 %collective-permute-done.9.refs_2_ = bf16[512,128]{1,0:T(8,128)(2,1)S(1)} collective-permute-done((bf16[512,128]{1,0:T(8,128)(2,1)S(1)}, bf16[512,128]{1,0:T(8,128)(2,1)S(1)}, u32[]{:S(2)}, u32[]{:S(2)}) %collective-permute-start.9) | collective-permute-done | bytes 131104 | tf_op jit(solution)/shard_map/ppermute | solution.py:223
  48.7 0.1 join_pieces.11
  48.8 3.0 %collective-permute-start.10 = (bf16[512,128]{1,0:T(8,128)(2,1)S(1)}, bf16[512,128]{1,0:T(8,128)(2,1)S(1)}, u32[]{:S(2)}, u32[]{:S(2)}) collective-permute-start(bf16[512,128]{1,0:T(8,128)(2,1)S(1)} %join_pieces.11), channel_id=1, source_target_pairs={{0,448},{32,480},{64,0},{96,32},{128,64},{160,96},{192,128},{224,1... | collective-permute-start | bytes 393224 | tf_op jit(solution)/shard_map/ppermute | solution.py:223
  51.8 0.0 copy-done
  51.8 0.2 fusion
  52.0 0.1 pad_add_fusion.place_ref
  52.0 0.0 collective-permute-done.6.refs_3_
  52.1 3.6 %collective-permute-done.10.refs_4_ = bf16[512,128]{1,0:T(8,128)(2,1)S(1)} collective-permute-done((bf16[512,128]{1,0:T(8,128)(2,1)S(1)}, bf16[512,128]{1,0:T(8,128)(2,1)S(1)}, u32[]{:S(2)}, u32[]{:S(2)}) %collective-permute-start.10) | collective-permute-done | bytes 131104 | tf_op jit(solution)/shard_map/ppermute | solution.py:223
  55.7 0.1 join_all.1
  55.8 13.6 %all_gather.3.block_ref = bf16[512,512]{1,0:T(8,128)(2,1)S(1)} all-gather(bf16[512,128]{1,0:T(8,128)(2,1)S(1)} %join_all.1), channel_id=1, replica_groups={{0,1,2,3},{4,5,6,7},{8,9,10,11},{12,13,14,15},{16,17,18,19},{20,21,22,2..., dimensions={1}, use_global_device_ids=true | all-gather | bytes 655360 | tf_op jit(solution)/shard_map/all_gather | solution.py:254
  69.3 6.4 %block_roots.1 = (bf16[512,128]{1,0:T(8,128)(2,1)}, bf16[2,512,512]{2,1,0:T(8,128)(2,1)}) custom-call(s32[3]{0:T(128)S(1)} %pad_add_fusion.place_ref, bf16[512,512]{1,0:T(8,128)(2,1)S(1)} %all_gather.3.block_ref), custom_call_target="tpu_custom_call" | custom-call | flops 4160749568 | bytes 2097152 | tf_op jit(solution)/shard_map/block_roots/pallas_call | solution.py:139
  (4 shorter events, 0.1 us)
Async XLA Ops:
  3.0 21.8 %collective-permute-start.2 = (bf16[1024,128]{1,0:T(8,128)(2,1)S(1)}, bf16[1024,128]{1,0:T(8,128)(2,1)S(1)}, u32[]{:S(2)}, u32[]{:S(2)}) collective-permute-start(bf16[1024,128]{1,0:T(8,128)(2,1)S(1)} %pad_maximum_fusion.2), channel_id=1, source_target_pairs={{0,32},{32,64},{64,96},{96,128},{128,160},{160,192},{192,224},{224... | collective-permute-start | bytes 786440 | tf_op jit(solution)/shard_map/ppermute | solution.py:223
  7.4 19.4 %collective-permute-start.7 = (bf16[1024,128]{1,0:T(8,128)(2,1)S(1)}, bf16[1024,128]{1,0:T(8,128)(2,1)S(1)}, u32[]{:S(2)}, u32[]{:S(2)}) collective-permute-start(bf16[1024,128]{1,0:T(8,128)(2,1)S(1)} %pad_maximum_fusion.3), channel_id=1, source_target_pairs={{0,480},{32,0},{64,32},{96,64},{128,96},{160,128},{192,160},{224,1... | collective-permute-start | bytes 786440 | tf_op jit(solution)/shard_map/ppermute | solution.py:223
  16.9 7.9 %collective-permute-start.3 = (bf16[512,128]{1,0:T(8,128)(2,1)S(1)}, bf16[512,128]{1,0:T(8,128)(2,1)S(1)}, u32[]{:S(2)}, u32[]{:S(2)}) collective-permute-start(bf16[512,128]{1,0:T(8,128)(2,1)S(1)} %get-tuple-element.11), channel_id=1, source_target_pairs={{0,64},{32,480},{64,128},{96,32},{128,192},{160,96},{192,256},{224... | collective-permute-start | bytes 393224 | tf_op jit(solution)/shard_map/ppermute | solution.py:223
  18.9 24.9 %collective-permute-start.1 = (bf16[1024,128]{1,0:T(8,128)(2,1)S(1)}, bf16[1024,128]{1,0:T(8,128)(2,1)S(1)}, u32[]{:S(2)}, u32[]{:S(2)}) collective-permute-start(bf16[1024,128]{1,0:T(8,128)(2,1)S(1)} %pad_maximum_fusion.1), channel_id=1, source_target_pairs={{0,32},{32,64},{64,96},{96,128},{128,160},{160,192},{192,224},{224... | collective-permute-start | bytes 786440 | tf_op jit(solution)/shard_map/ppermute | solution.py:223
  24.8 27.0 %copy-start = (s32[1,8,2]{1,2,0:T(2,128)S(1)}, s32[1,8,2]{1,2,0:T(2,128)}, u32[]{:S(2)}) copy-start(s32[1,8,2]{1,2,0:T(2,128)} %param.3) | copy-start | bytes 196
  24.9 9.8 %collective-permute-start.4 = (bf16[512,128]{1,0:T(8,128)(2,1)S(1)}, bf16[512,128]{1,0:T(8,128)(2,1)S(1)}, u32[]{:S(2)}, u32[]{:S(2)}) collective-permute-start(bf16[512,128]{1,0:T(8,128)(2,1)S(1)} %join_pieces.6), channel_id=1, source_target_pairs={{0,64},{32,96},{64,128},{96,160},{128,192},{160,224},{192,256},{22... | collective-permute-start | bytes 393224 | tf_op jit(solution)/shard_map/ppermute | solution.py:223
  26.9 10.5 %collective-permute-start.8 = (bf16[512,128]{1,0:T(8,128)(2,1)S(1)}, bf16[512,128]{1,0:T(8,128)(2,1)S(1)}, u32[]{:S(2)}, u32[]{:S(2)}) collective-permute-start(bf16[512,128]{1,0:T(8,128)(2,1)S(1)} %join_pieces.9), channel_id=1, source_target_pairs={{0,448},{32,480},{64,0},{96,32},{128,64},{160,96},{192,128},{224,1... | collective-permute-start | bytes 393224 | tf_op jit(solution)/shard_map/ppermute | solution.py:223
  32.4 13.4 %collective-permute-start = (bf16[1024,128]{1,0:T(8,128)(2,1)S(1)}, bf16[1024,128]{1,0:T(8,128)(2,1)S(1)}, u32[]{:S(2)}, u32[]{:S(2)}) collective-permute-start(bf16[1024,128]{1,0:T(8,128)(2,1)S(1)} %pad_maximum_fusion), channel_id=1, source_target_pairs={{0,480},{32,0},{64,32},{96,64},{128,96},{160,128},{192,160},{224,1... | collective-permute-start | bytes 786440 | tf_op jit(solution)/shard_map/ppermute | solution.py:223
  34.7 9.1 %collective-permute-start.5 = (bf16[512,128]{1,0:T(8,128)(2,1)S(1)}, bf16[512,128]{1,0:T(8,128)(2,1)S(1)}, u32[]{:S(2)}, u32[]{:S(2)}) collective-permute-start(bf16[512,128]{1,0:T(8,128)(2,1)S(1)} %join_pieces.7), channel_id=1, source_target_pairs={{0,64},{32,96},{64,128},{96,160},{128,192},{160,224},{192,256},{22... | collective-permute-start | bytes 393224 | tf_op jit(solution)/shard_map/ppermute | solution.py:223
  37.4 11.3 %collective-permute-start.9 = (bf16[512,128]{1,0:T(8,128)(2,1)S(1)}, bf16[512,128]{1,0:T(8,128)(2,1)S(1)}, u32[]{:S(2)}, u32[]{:S(2)}) collective-permute-start(bf16[512,128]{1,0:T(8,128)(2,1)S(1)} %join_pieces.10), channel_id=1, source_target_pairs={{0,448},{32,480},{64,0},{96,32},{128,64},{160,96},{192,128},{224,1... | collective-permute-start | bytes 393224 | tf_op jit(solution)/shard_map/ppermute | solution.py:223
  43.8 8.2 %collective-permute-start.6 = (bf16[512,128]{1,0:T(8,128)(2,1)S(1)}, bf16[512,128]{1,0:T(8,128)(2,1)S(1)}, u32[]{:S(2)}, u32[]{:S(2)}) collective-permute-start(bf16[512,128]{1,0:T(8,128)(2,1)S(1)} %join_pieces.8), channel_id=1, source_target_pairs={{0,64},{32,96},{64,128},{96,160},{128,192},{160,224},{192,256},{22... | collective-permute-start | bytes 393224 | tf_op jit(solution)/shard_map/ppermute | solution.py:223
  48.8 6.9 %collective-permute-start.10 = (bf16[512,128]{1,0:T(8,128)(2,1)S(1)}, bf16[512,128]{1,0:T(8,128)(2,1)S(1)}, u32[]{:S(2)}, u32[]{:S(2)}) collective-permute-start(bf16[512,128]{1,0:T(8,128)(2,1)S(1)} %join_pieces.11), channel_id=1, source_target_pairs={{0,448},{32,480},{64,0},{96,32},{128,64},{160,96},{192,128},{224,1... | collective-permute-start | bytes 393224 | tf_op jit(solution)/shard_map/ppermute | solution.py:223

commit v6 on v5

--- a/solution.py
+++ b/solution.py
@@ -171,10 +171,10 @@
     (1, (3, 1)),
     (2, (6,)),
     (-2, (-6,)),
-    (-2, (-4,)),
-    (2, (4,)),
+    (-2, (-2,)),
     (2, (2,)),
-    (-2, (-2,)),
+    (4, (4,)),
+    (-4, (-4,)),
 )
 
 
@@ -211,16 +211,23 @@
 
 def summed_piece(grads):
     size = lax.axis_size("dp")
+    columns = lax.axis_size("work")
     place = lax.axis_index("dp")
+    side = 1 - 2 * (lax.axis_index("work") % 2)
     pieces = grads.reshape(size, grads.shape[0] // size, grads.shape[1])
     rows = pieces.shape[1]
     parity = (place % 2)[None].astype(jnp.int32)
 
     def own(distance):
-        return lax.dynamic_index_in_dim(pieces, (place + distance) % size, 0, keepdims=False)
+        return lax.dynamic_index_in_dim(pieces, (place + side * distance) % size, 0, keepdims=False)
 
     def moved(value, shift):
-        return lax.ppermute(value, "dp", [(i, (i + shift(i)) % size) for i in range(size)])
+        pairs = [
+            (i * columns + w, (i + (1 - 2 * (w % 2)) * shift(i)) % size * columns + w)
+            for i in range(size)
+            for w in range(columns)
+        ]
+        return lax.ppermute(value, ("dp", "work"), pairs)
 
     terms = {distance: [(own(distance), 0, None)] for distance in range(-7, 8)}
     for step in ROUTE:

time: 76.2 us -> 74.2 us (0.974)
  the two profiles are of different devices: /device:TPU:1 before, /device:TPU:41 now
where the time goes in v6:
time: 74.2 us; the launch traced here: 73.8 us
  starting transfers between devices  43.3 us (58%)
  waiting for transfers between devices  11 us (15%)
  blocking collectives  8.92 us (12%)
  Pallas kernels  6.85 us (9%)
  local copies, waits for them, and re-layouts  2.09 us (3%)
  between operations  1.26 us (2%)
    ppermute x11, starting transfers between devices, moved(): return lax.ppermute(value, ('dp', 'work'), pairs)  43.3 us
    ppermute x11, waiting for transfers between devices, moved(): return lax.ppermute(value, ('dp', 'work'), pairs)  11 us
    all_gather x1, blocking collectives, local(): lax.all_gather(summed, 'work', axis=1, tiled=True, axis_index_groups=groups)  8.92 us
    pallas_call x1, Pallas kernels, block_call(): pl.pallas_call(block_kernel, out_shape=(jax.ShapeDtypeStruct((order, widt...  6.43 us
    squeeze x1, local copies, waits for them, and re-layouts, own(): lax.dynamic_index_in_dim(pieces, (place + side * distance) % size, 0, kee...  2.08 us
  transfers between devices with their start and end apart: 11, of which 2 were waited for; matrix products, arithmetic and copies ran while one was open for 0% of the time, Pallas kernels for 0%

profile of v6, /device:TPU:41, one launch (start us, length us, event | category | flops | bytes accessed | tf_op | source)
XLA Modules:
  0.0 73.8 jit_solution(11260613510200909962)
XLA Ops:
  1.0 2.1 %dynamic-slice_bitcast_fusion = (bf16[512,128]{1,0:T(8,128)(2,1)S(1)}, bf16[512,128]{1,0:T(8,128)(2,1)S(1)}, bf16[512,128]{1,0:T(8,128)(2,1)S(1)}, bf16[512,128]...) fusion(bf16[16,512,128]{2,1,0:T(8,128)(2,1)} %bitcast.36, ...), kind=kLoop, calls=%fused_computation.4 | loop fusion | bytes 4194368 | tf_op jit(solution)/shard_map/jit(dynamic_index_in_dim)/squeeze | solution.py:222
  3.1 4.9 %collective-permute-start.5 = (bf16[512,128]{1,0:T(8,128)(2,1)S(1)}, bf16[512,128]{1,0:T(8,128)(2,1)S(1)}, u32[]{:S(2)}, u32[]{:S(2)}) collective-permute-start(bf16[512,128]{1,0:T(8,128)(2,1)S(1)} %get-tuple-element.10), channel_id=1, source_target_pairs={{0,64},{1,449},{2,66},{3,451},{4,68},{5,453},{6,70},{7,455},{8,72}... | collective-permute-start | bytes 393224 | tf_op jit(solution)/shard_map/ppermute | solution.py:230
  8.0 8.4 %collective-permute-start.4 = (bf16[1024,128]{1,0:T(8,128)(2,1)S(1)}, bf16[1024,128]{1,0:T(8,128)(2,1)S(1)}, u32[]{:S(2)}, u32[]{:S(2)}) collective-permute-start(bf16[1024,128]{1,0:T(8,128)(2,1)S(1)} %pad_maximum_fusion.2), channel_id=1, source_target_pairs={{0,32},{1,481},{2,34},{3,483},{4,36},{5,485},{6,38},{7,487},{8,40}... | collective-permute-start | bytes 786440 | tf_op jit(solution)/shard_map/ppermute | solution.py:230
  16.4 1.9 %collective-permute-start.8 = (bf16[1024,128]{1,0:T(8,128)(2,1)S(1)}, bf16[1024,128]{1,0:T(8,128)(2,1)S(1)}, u32[]{:S(2)}, u32[]{:S(2)}) collective-permute-start(bf16[1024,128]{1,0:T(8,128)(2,1)S(1)} %pad_maximum_fusion.3), channel_id=1, source_target_pairs={{0,480},{1,33},{2,482},{3,35},{4,484},{5,37},{6,486},{7,39},{8,488... | collective-permute-start | bytes 786440 | tf_op jit(solution)/shard_map/ppermute | solution.py:230
  18.4 1.9 %collective-permute-start = (bf16[1024,128]{1,0:T(8,128)(2,1)S(1)}, bf16[1024,128]{1,0:T(8,128)(2,1)S(1)}, u32[]{:S(2)}, u32[]{:S(2)}) collective-permute-start(bf16[1024,128]{1,0:T(8,128)(2,1)S(1)} %pad_maximum_fusion), channel_id=1, source_target_pairs={{0,480},{1,33},{2,482},{3,35},{4,484},{5,37},{6,486},{7,39},{8,488... | collective-permute-start | bytes 786440 | tf_op jit(solution)/shard_map/ppermute | solution.py:230
  20.3 0.0 copy-start
  20.4 3.4 %collective-permute-start.1 = (bf16[1024,128]{1,0:T(8,128)(2,1)S(1)}, bf16[1024,128]{1,0:T(8,128)(2,1)S(1)}, u32[]{:S(2)}, u32[]{:S(2)}) collective-permute-start(bf16[1024,128]{1,0:T(8,128)(2,1)S(1)} %pad_maximum_fusion.1), channel_id=1, source_target_pairs={{0,32},{1,481},{2,34},{3,483},{4,36},{5,485},{6,38},{7,487},{8,40}... | collective-permute-start | bytes 786440 | tf_op jit(solution)/shard_map/ppermute | solution.py:230
  23.7 0.0 collective-permute-done.5.refs_2_
  23.8 0.0 collective-permute-done.4.refs_1_
  23.8 0.1 join_pieces.8
  23.8 4.3 %collective-permute-start.6 = (bf16[512,128]{1,0:T(8,128)(2,1)S(1)}, bf16[512,128]{1,0:T(8,128)(2,1)S(1)}, u32[]{:S(2)}, u32[]{:S(2)}) collective-permute-start(bf16[512,128]{1,0:T(8,128)(2,1)S(1)} %join_pieces.8), channel_id=1, source_target_pairs={{0,64},{1,449},{2,66},{3,451},{4,68},{5,453},{6,70},{7,455},{8,72}... | collective-permute-start | bytes 393224 | tf_op jit(solution)/shard_map/ppermute | solution.py:230
  28.1 0.0 collective-permute-done.8.refs_1_
  28.2 0.1 join_pieces.10
  28.2 1.9 %collective-permute-start.9 = (bf16[512,128]{1,0:T(8,128)(2,1)S(1)}, bf16[512,128]{1,0:T(8,128)(2,1)S(1)}, u32[]{:S(2)}, u32[]{:S(2)}) collective-permute-start(bf16[512,128]{1,0:T(8,128)(2,1)S(1)} %join_pieces.10), channel_id=1, source_target_pairs={{0,448},{1,65},{2,450},{3,67},{4,452},{5,69},{6,454},{7,71},{8,456... | collective-permute-start | bytes 393224 | tf_op jit(solution)/shard_map/ppermute | solution.py:230
  30.2 0.0 collective-permute-done.refs_1_
  30.2 3.4 %collective-permute-start.2 = (bf16[512,128]{1,0:T(8,128)(2,1)S(1)}, bf16[512,128]{1,0:T(8,128)(2,1)S(1)}, u32[]{:S(2)}, u32[]{:S(2)}) collective-permute-start(bf16[512,128]{1,0:T(8,128)(2,1)S(1)} %join_pieces.6), channel_id=1, source_target_pairs={{0,448},{1,65},{2,450},{3,67},{4,452},{5,69},{6,454},{7,71},{8,456... | collective-permute-start | bytes 393224 | tf_op jit(solution)/shard_map/ppermute | solution.py:230
  33.7 0.0 collective-permute-done.1.refs_1_.refs_2_
  33.7 3.9 %collective-permute-start.3 = (bf16[512,128]{1,0:T(8,128)(2,1)S(1)}, bf16[512,128]{1,0:T(8,128)(2,1)S(1)}, u32[]{:S(2)}, u32[]{:S(2)}) collective-permute-start(bf16[512,128]{1,0:T(8,128)(2,1)S(1)} %join_pieces.7), channel_id=1, source_target_pairs={{0,64},{1,449},{2,66},{3,451},{4,68},{5,453},{6,70},{7,455},{8,72}... | collective-permute-start | bytes 393224 | tf_op jit(solution)/shard_map/ppermute | solution.py:230
  37.7 0.0 collective-permute-done.6.refs_2_
  37.7 0.1 join_pieces.9
  37.7 5.9 %collective-permute-start.7 = (bf16[512,128]{1,0:T(8,128)(2,1)S(1)}, bf16[512,128]{1,0:T(8,128)(2,1)S(1)}, u32[]{:S(2)}, u32[]{:S(2)}) collective-permute-start(bf16[512,128]{1,0:T(8,128)(2,1)S(1)} %join_pieces.9), channel_id=1, source_target_pairs={{0,128},{1,385},{2,130},{3,387},{4,132},{5,389},{6,134},{7,391},{8... | collective-permute-start | bytes 393224 | tf_op jit(solution)/shard_map/ppermute | solution.py:230
  43.7 0.0 collective-permute-done.9.refs_2_
  43.7 0.1 join_pieces.11
  43.7 3.3 %collective-permute-start.10 = (bf16[512,128]{1,0:T(8,128)(2,1)S(1)}, bf16[512,128]{1,0:T(8,128)(2,1)S(1)}, u32[]{:S(2)}, u32[]{:S(2)}) collective-permute-start(bf16[512,128]{1,0:T(8,128)(2,1)S(1)} %join_pieces.11), channel_id=1, source_target_pairs={{0,384},{1,129},{2,386},{3,131},{4,388},{5,133},{6,390},{7,135},{8... | collective-permute-start | bytes 393224 | tf_op jit(solution)/shard_map/ppermute | solution.py:230
  47.0 0.0 copy-done
  47.0 0.2 fusion
  47.2 0.1 pad_add_fusion.place_ref
  47.3 0.0 collective-permute-done.2.refs_3_
  47.3 0.0 collective-permute-done.3.refs_4_
  47.3 2.1 %collective-permute-done.7.refs_5_ = bf16[512,128]{1,0:T(8,128)(2,1)S(1)} collective-permute-done((bf16[512,128]{1,0:T(8,128)(2,1)S(1)}, bf16[512,128]{1,0:T(8,128)(2,1)S(1)}, u32[]{:S(2)}, u32[]{:S(2)}) %collective-permute-start.7) | collective-permute-done | bytes 131104 | tf_op jit(solution)/shard_map/ppermute | solution.py:230
  49.4 8.9 %collective-permute-done.10.refs_6_ = bf16[512,128]{1,0:T(8,128)(2,1)S(1)} collective-permute-done((bf16[512,128]{1,0:T(8,128)(2,1)S(1)}, bf16[512,128]{1,0:T(8,128)(2,1)S(1)}, u32[]{:S(2)}, u32[]{:S(2)}) %collective-permute-start.10) | collective-permute-done | bytes 131104 | tf_op jit(solution)/shard_map/ppermute | solution.py:230
  58.3 0.1 join_all.1
  58.4 8.9 %all_gather.3.block_ref = bf16[512,512]{1,0:T(8,128)(2,1)S(1)} all-gather(bf16[512,128]{1,0:T(8,128)(2,1)S(1)} %join_all.1), channel_id=1, replica_groups={{0,1,2,3},{4,5,6,7},{8,9,10,11},{12,13,14,15},{16,17,18,19},{20,21,22,2..., dimensions={1}, use_global_device_ids=true | all-gather | bytes 655360 | tf_op jit(solution)/shard_map/all_gather | solution.py:261
  67.3 6.4 %block_roots.1 = (bf16[512,128]{1,0:T(8,128)(2,1)}, bf16[2,512,512]{2,1,0:T(8,128)(2,1)}) custom-call(s32[3]{0:T(128)S(1)} %pad_add_fusion.place_ref, bf16[512,512]{1,0:T(8,128)(2,1)S(1)} %all_gather.3.block_ref), custom_call_target="tpu_custom_call" | custom-call | flops 4160749568 | bytes 2097152 | tf_op jit(solution)/shard_map/block_roots/pallas_call | solution.py:139
  (6 shorter events, 0.1 us)
Async XLA Ops:
  3.1 20.7 %collective-permute-start.5 = (bf16[512,128]{1,0:T(8,128)(2,1)S(1)}, bf16[512,128]{1,0:T(8,128)(2,1)S(1)}, u32[]{:S(2)}, u32[]{:S(2)}) collective-permute-start(bf16[512,128]{1,0:T(8,128)(2,1)S(1)} %get-tuple-element.10), channel_id=1, source_target_pairs={{0,64},{1,449},{2,66},{3,451},{4,68},{5,453},{6,70},{7,455},{8,72}... | collective-permute-start | bytes 393224 | tf_op jit(solution)/shard_map/ppermute | solution.py:230
  8.0 15.8 %collective-permute-start.4 = (bf16[1024,128]{1,0:T(8,128)(2,1)S(1)}, bf16[1024,128]{1,0:T(8,128)(2,1)S(1)}, u32[]{:S(2)}, u32[]{:S(2)}) collective-permute-start(bf16[1024,128]{1,0:T(8,128)(2,1)S(1)} %pad_maximum_fusion.2), channel_id=1, source_target_pairs={{0,32},{1,481},{2,34},{3,483},{4,36},{5,485},{6,38},{7,487},{8,40}... | collective-permute-start | bytes 786440 | tf_op jit(solution)/shard_map/ppermute | solution.py:230
  16.4 11.7 %collective-permute-start.8 = (bf16[1024,128]{1,0:T(8,128)(2,1)S(1)}, bf16[1024,128]{1,0:T(8,128)(2,1)S(1)}, u32[]{:S(2)}, u32[]{:S(2)}) collective-permute-start(bf16[1024,128]{1,0:T(8,128)(2,1)S(1)} %pad_maximum_fusion.3), channel_id=1, source_target_pairs={{0,480},{1,33},{2,482},{3,35},{4,484},{5,37},{6,486},{7,39},{8,488... | collective-permute-start | bytes 786440 | tf_op jit(solution)/shard_map/ppermute | solution.py:230
  18.4 11.8 %collective-permute-start = (bf16[1024,128]{1,0:T(8,128)(2,1)S(1)}, bf16[1024,128]{1,0:T(8,128)(2,1)S(1)}, u32[]{:S(2)}, u32[]{:S(2)}) collective-permute-start(bf16[1024,128]{1,0:T(8,128)(2,1)S(1)} %pad_maximum_fusion), channel_id=1, source_target_pairs={{0,480},{1,33},{2,482},{3,35},{4,484},{5,37},{6,486},{7,39},{8,488... | collective-permute-start | bytes 786440 | tf_op jit(solution)/shard_map/ppermute | solution.py:230
  20.3 26.7 %copy-start = (s32[1,8,2]{1,2,0:T(2,128)S(1)}, s32[1,8,2]{1,2,0:T(2,128)}, u32[]{:S(2)}) copy-start(s32[1,8,2]{1,2,0:T(2,128)} %param.3) | copy-start | bytes 196
  20.4 13.3 %collective-permute-start.1 = (bf16[1024,128]{1,0:T(8,128)(2,1)S(1)}, bf16[1024,128]{1,0:T(8,128)(2,1)S(1)}, u32[]{:S(2)}, u32[]{:S(2)}) collective-permute-start(bf16[1024,128]{1,0:T(8,128)(2,1)S(1)} %pad_maximum_fusion.1), channel_id=1, source_target_pairs={{0,32},{1,481},{2,34},{3,483},{4,36},{5,485},{6,38},{7,487},{8,40}... | collective-permute-start | bytes 786440 | tf_op jit(solution)/shard_map/ppermute | solution.py:230
  23.8 13.8 %collective-permute-start.6 = (bf16[512,128]{1,0:T(8,128)(2,1)S(1)}, bf16[512,128]{1,0:T(8,128)(2,1)S(1)}, u32[]{:S(2)}, u32[]{:S(2)}) collective-permute-start(bf16[512,128]{1,0:T(8,128)(2,1)S(1)} %join_pieces.8), channel_id=1, source_target_pairs={{0,64},{1,449},{2,66},{3,451},{4,68},{5,453},{6,70},{7,455},{8,72}... | collective-permute-start | bytes 393224 | tf_op jit(solution)/shard_map/ppermute | solution.py:230
  28.2 15.4 %collective-permute-start.9 = (bf16[512,128]{1,0:T(8,128)(2,1)S(1)}, bf16[512,128]{1,0:T(8,128)(2,1)S(1)}, u32[]{:S(2)}, u32[]{:S(2)}) collective-permute-start(bf16[512,128]{1,0:T(8,128)(2,1)S(1)} %join_pieces.10), channel_id=1, source_target_pairs={{0,448},{1,65},{2,450},{3,67},{4,452},{5,69},{6,454},{7,71},{8,456... | collective-permute-start | bytes 393224 | tf_op jit(solution)/shard_map/ppermute | solution.py:230
  30.2 17.1 %collective-permute-start.2 = (bf16[512,128]{1,0:T(8,128)(2,1)S(1)}, bf16[512,128]{1,0:T(8,128)(2,1)S(1)}, u32[]{:S(2)}, u32[]{:S(2)}) collective-permute-start(bf16[512,128]{1,0:T(8,128)(2,1)S(1)} %join_pieces.6), channel_id=1, source_target_pairs={{0,448},{1,65},{2,450},{3,67},{4,452},{5,69},{6,454},{7,71},{8,456... | collective-permute-start | bytes 393224 | tf_op jit(solution)/shard_map/ppermute | solution.py:230
  33.7 13.6 %collective-permute-start.3 = (bf16[512,128]{1,0:T(8,128)(2,1)S(1)}, bf16[512,128]{1,0:T(8,128)(2,1)S(1)}, u32[]{:S(2)}, u32[]{:S(2)}) collective-permute-start(bf16[512,128]{1,0:T(8,128)(2,1)S(1)} %join_pieces.7), channel_id=1, source_target_pairs={{0,64},{1,449},{2,66},{3,451},{4,68},{5,453},{6,70},{7,455},{8,72}... | collective-permute-start | bytes 393224 | tf_op jit(solution)/shard_map/ppermute | solution.py:230
  37.7 11.7 %collective-permute-start.7 = (bf16[512,128]{1,0:T(8,128)(2,1)S(1)}, bf16[512,128]{1,0:T(8,128)(2,1)S(1)}, u32[]{:S(2)}, u32[]{:S(2)}) collective-permute-start(bf16[512,128]{1,0:T(8,128)(2,1)S(1)} %join_pieces.9), channel_id=1, source_target_pairs={{0,128},{1,385},{2,130},{3,387},{4,132},{5,389},{6,134},{7,391},{8... | collective-permute-start | bytes 393224 | tf_op jit(solution)/shard_map/ppermute | solution.py:230
  43.7 14.6 %collective-permute-start.10 = (bf16[512,128]{1,0:T(8,128)(2,1)S(1)}, bf16[512,128]{1,0:T(8,128)(2,1)S(1)}, u32[]{:S(2)}, u32[]{:S(2)}) collective-permute-start(bf16[512,128]{1,0:T(8,128)(2,1)S(1)} %join_pieces.11), channel_id=1, source_target_pairs={{0,384},{1,129},{2,386},{3,131},{4,388},{5,133},{6,390},{7,135},{8... | collective-permute-start | bytes 393224 | tf_op jit(solution)/shard_map/ppermute | solution.py:230

commit v7 on v6

--- a/solution.py
+++ b/solution.py
@@ -209,6 +209,42 @@
     )(parity, *arrays)
 
 
+def fetch_kernel(groups, size, where_ref, pieces_ref, *refs):
+    *out_refs, done = refs
+    rows = pieces_ref.shape[1]
+    copies = []
+    for out_ref, distances in zip(out_refs, groups):
+        for order, distance in enumerate(distances):
+            index = lax.rem(where_ref[0] + where_ref[1] * distance + size, size)
+            copies.append(
+                pltpu.make_async_copy(
+                    pieces_ref.at[index],
+                    out_ref.at[pl.ds(order * rows, rows), :],
+                    done.at[len(copies)],
+                )
+            )
+    for copy in copies:
+        copy.start()
+    for copy in copies:
+        copy.wait()
+
+
+def fetch(where, pieces, groups):
+    size, rows, width = pieces.shape
+    return pl.pallas_call(
+        functools.partial(fetch_kernel, groups, size),
+        out_shape=[jax.ShapeDtypeStruct((len(g) * rows, width), pieces.dtype) for g in groups],
+        in_specs=[pl.BlockSpec(memory_space=pltpu.SMEM), pl.BlockSpec(memory_space=pl.ANY)],
+        out_specs=[pl.BlockSpec(memory_space=pltpu.VMEM)] * len(groups),
+        scratch_shapes=[pltpu.SemaphoreType.DMA((sum(len(g) for g in groups),))],
+        compiler_params=pltpu.CompilerParams(vmem_limit_bytes=50 * 1024 * 1024),
+        cost_estimate=pl.CostEstimate(
+            flops=0, bytes_accessed=4 * size * rows * width, transcendentals=0
+        ),
+        name="fetch_pieces",
+    )(where, pieces)
+
+
 def summed_piece(grads):
     size = lax.axis_size("dp")
     columns = lax.axis_size("work")
@@ -218,9 +254,6 @@
     rows = pieces.shape[1]
     parity = (place % 2)[None].astype(jnp.int32)
 
-    def own(distance):
-        return lax.dynamic_index_in_dim(pieces, (place + side * distance) % size, 0, keepdims=False)
-
     def moved(value, shift):
         pairs = [
             (i * columns + w, (i + (1 - 2 * (w % 2)) * shift(i)) % size * columns + w)
@@ -229,20 +262,30 @@
         ]
         return lax.ppermute(value, ("dp", "work"), pairs)
 
-    terms = {distance: [(own(distance), 0, None)] for distance in range(-7, 8)}
+    messages, joined = [(-8,)], {6, -6}
+    for step in ROUTE:
+        if step != OPPOSITE:
+            shift, distances = step
+            if not joined.intersection(distances):
+                messages.append(distances)
+            joined.update(distance - shift for distance in distances)
+    kept = [(distance,) for distance in range(-7, 8) if distance in joined]
+    where = jnp.stack([place, side]).astype(jnp.int32)
+    fetched = dict(zip(messages + kept, fetch(where, pieces, messages + kept)))
+
+    terms = {distance: [(fetched[(distance,)], 0, None)] for (distance,) in kept}
     for step in ROUTE:
         if step == OPPOSITE:
-            arrived = moved(own(-8), lambda i: 2 if i % 2 == 0 else -2)
+            arrived = moved(fetched[(-8,)], lambda i: 2 if i % 2 == 0 else -2)
             terms[6].append((arrived, 0, 0))
             terms[-6].append((arrived, 0, 1))
             continue
         shift, distances = step
-        leaving = [terms.pop(distance) for distance in distances]
-        if all(len(parts) == 1 for parts in leaving):
-            value = jnp.concatenate([parts[0][0] for parts in leaving], 0)
+        if distances in messages:
+            value = fetched[distances]
         else:
-            (parts,) = leaving
-            value = join(parity, rows, "join_pieces", parts)
+            (distance,) = distances
+            value = join(parity, rows, "join_pieces", terms.pop(distance))
         arrived = moved(value, lambda i, shift=shift: shift)
         for order, distance in enumerate(distances):
             terms[distance - shift].append((arrived, order * rows, None))

time: 74.2 us -> 79.1 us (1.066)
  the two profiles are of different devices: /device:TPU:41 before, /device:TPU:1 now
where the time goes in v7:
time: 79.1 us; the launch traced here: 78.7 us
  starting transfers between devices  48 us (61%)
  waiting for transfers between devices  13 us (16%)
  Pallas kernels  9.15 us (12%)
  blocking collectives  7.31 us (9%)
  between operations  0.87 us (1%)
    ppermute x11, starting transfers between devices, moved(): return lax.ppermute(value, ('dp', 'work'), pairs)  48 us
    ppermute x11, waiting for transfers between devices, moved(): return lax.ppermute(value, ('dp', 'work'), pairs)  13 us
    all_gather x1, blocking collectives, local(): lax.all_gather(summed, 'work', axis=1, tiled=True, axis_index_groups=groups)  7.31 us
    pallas_call x1, Pallas kernels, block_call(): pl.pallas_call(block_kernel, out_shape=(jax.ShapeDtypeStruct((order, widt...  6.43 us
    pallas_call x1, Pallas kernels, fetch(): pl.pallas_call(functools.partial(fetch_kernel, groups, size), out_shape=[...  2.29 us
  transfers between devices with their start and end apart: 11, of which 3 were waited for; matrix products, arithmetic and copies ran while one was open for 0% of the time, Pallas kernels for 0%

profile of v7, /device:TPU:1, one launch (start us, length us, event | category | flops | bytes accessed | tf_op | source)
XLA Modules:
  0.0 78.7 jit_solution(17203191142415374546)
XLA Ops:
  0.6 0.1 pad_add_fusion.1.where_ref
  0.7 2.3 %fetch_pieces.1 = (bf16[512,128]{1,0:T(8,128)(2,1)S(1)}, bf16[1024,128]{1,0:T(8,128)(2,1)S(1)}, bf16[1024,128]{1,0:T(8,128)(2,1)S(1)}, bf16[1024,128]{1,0:T(8,12...) custom-call(s32[2]{0:T(128)S(1)} %pad_add_fusion.1.where_ref, ...), custom_call_target="tpu_custom_call" | custom-call | bytes 4194304 | tf_op jit(solution)/shard_map/fetch_pieces/pallas_call | solution.py:234
  3.0 0.0 copy-start
  3.0 12.0 %collective-permute-start.4 = (bf16[1024,128]{1,0:T(8,128)(2,1)S(1)}, bf16[1024,128]{1,0:T(8,128)(2,1)S(1)}, u32[]{:S(2)}, u32[]{:S(2)}) collective-permute-start(bf16[1024,128]{1,0:T(8,128)(2,1)S(1)} %get-tuple-element.22), channel_id=1, source_target_pairs={{0,32},{1,481},{2,34},{3,483},{4,36},{5,485},{6,38},{7,487},{8,40}... | collective-permute-start | bytes 786440 | tf_op jit(solution)/shard_map/ppermute | solution.py:263
  15.0 1.9 %collective-permute-start.8 = (bf16[1024,128]{1,0:T(8,128)(2,1)S(1)}, bf16[1024,128]{1,0:T(8,128)(2,1)S(1)}, u32[]{:S(2)}, u32[]{:S(2)}) collective-permute-start(bf16[1024,128]{1,0:T(8,128)(2,1)S(1)} %get-tuple-element.26), channel_id=1, source_target_pairs={{0,480},{1,33},{2,482},{3,35},{4,484},{5,37},{6,486},{7,39},{8,488... | collective-permute-start | bytes 786440 | tf_op jit(solution)/shard_map/ppermute | solution.py:263
  16.9 1.9 %collective-permute-start = (bf16[1024,128]{1,0:T(8,128)(2,1)S(1)}, bf16[1024,128]{1,0:T(8,128)(2,1)S(1)}, u32[]{:S(2)}, u32[]{:S(2)}) collective-permute-start(bf16[1024,128]{1,0:T(8,128)(2,1)S(1)} %get-tuple-element.17), channel_id=1, source_target_pairs={{0,480},{1,33},{2,482},{3,35},{4,484},{5,37},{6,486},{7,39},{8,488... | collective-permute-start | bytes 786440 | tf_op jit(solution)/shard_map/ppermute | solution.py:263
  18.8 5.7 %collective-permute-start.5 = (bf16[512,128]{1,0:T(8,128)(2,1)S(1)}, bf16[512,128]{1,0:T(8,128)(2,1)S(1)}, u32[]{:S(2)}, u32[]{:S(2)}) collective-permute-start(bf16[512,128]{1,0:T(8,128)(2,1)S(1)} %get-tuple-element.24), channel_id=1, source_target_pairs={{0,64},{1,449},{2,66},{3,451},{4,68},{5,453},{6,70},{7,455},{8,72}... | collective-permute-start | bytes 393224 | tf_op jit(solution)/shard_map/ppermute | solution.py:263
  24.6 1.9 %collective-permute-start.1 = (bf16[1024,128]{1,0:T(8,128)(2,1)S(1)}, bf16[1024,128]{1,0:T(8,128)(2,1)S(1)}, u32[]{:S(2)}, u32[]{:S(2)}) collective-permute-start(bf16[1024,128]{1,0:T(8,128)(2,1)S(1)} %get-tuple-element.18), channel_id=1, source_target_pairs={{0,32},{1,481},{2,34},{3,483},{4,36},{5,485},{6,38},{7,487},{8,40}... | collective-permute-start | bytes 786440 | tf_op jit(solution)/shard_map/ppermute | solution.py:263
  26.5 1.6 %collective-permute-done.5.refs_2_ = bf16[512,128]{1,0:T(8,128)(2,1)S(1)} collective-permute-done((bf16[512,128]{1,0:T(8,128)(2,1)S(1)}, bf16[512,128]{1,0:T(8,128)(2,1)S(1)}, u32[]{:S(2)}, u32[]{:S(2)}) %collective-permute-start.5) | collective-permute-done | bytes 131104 | tf_op jit(solution)/shard_map/ppermute | solution.py:263
  28.1 0.0 collective-permute-done.4.refs_1_
  28.1 0.1 join_pieces.8
  28.2 6.0 %collective-permute-start.6 = (bf16[512,128]{1,0:T(8,128)(2,1)S(1)}, bf16[512,128]{1,0:T(8,128)(2,1)S(1)}, u32[]{:S(2)}, u32[]{:S(2)}) collective-permute-start(bf16[512,128]{1,0:T(8,128)(2,1)S(1)} %join_pieces.8), channel_id=1, source_target_pairs={{0,64},{1,449},{2,66},{3,451},{4,68},{5,453},{6,70},{7,455},{8,72}... | collective-permute-start | bytes 393224 | tf_op jit(solution)/shard_map/ppermute | solution.py:263
  34.2 0.0 collective-permute-done.8.refs_1_
  34.2 0.1 join_pieces.10
  34.3 1.9 %collective-permute-start.9 = (bf16[512,128]{1,0:T(8,128)(2,1)S(1)}, bf16[512,128]{1,0:T(8,128)(2,1)S(1)}, u32[]{:S(2)}, u32[]{:S(2)}) collective-permute-start(bf16[512,128]{1,0:T(8,128)(2,1)S(1)} %join_pieces.10), channel_id=1, source_target_pairs={{0,448},{1,65},{2,450},{3,67},{4,452},{5,69},{6,454},{7,71},{8,456... | collective-permute-start | bytes 393224 | tf_op jit(solution)/shard_map/ppermute | solution.py:263
  36.2 0.0 collective-permute-done.refs_1_
  36.2 1.9 %collective-permute-start.2 = (bf16[512,128]{1,0:T(8,128)(2,1)S(1)}, bf16[512,128]{1,0:T(8,128)(2,1)S(1)}, u32[]{:S(2)}, u32[]{:S(2)}) collective-permute-start(bf16[512,128]{1,0:T(8,128)(2,1)S(1)} %join_pieces.6), channel_id=1, source_target_pairs={{0,448},{1,65},{2,450},{3,67},{4,452},{5,69},{6,454},{7,71},{8,456... | collective-permute-start | bytes 393224 | tf_op jit(solution)/shard_map/ppermute | solution.py:263
  38.2 0.0 collective-permute-done.1.refs_1_.refs_2_
  38.2 5.5 %collective-permute-start.3 = (bf16[512,128]{1,0:T(8,128)(2,1)S(1)}, bf16[512,128]{1,0:T(8,128)(2,1)S(1)}, u32[]{:S(2)}, u32[]{:S(2)}) collective-permute-start(bf16[512,128]{1,0:T(8,128)(2,1)S(1)} %join_pieces.7), channel_id=1, source_target_pairs={{0,64},{1,449},{2,66},{3,451},{4,68},{5,453},{6,70},{7,455},{8,72}... | collective-permute-start | bytes 393224 | tf_op jit(solution)/shard_map/ppermute | solution.py:263
  43.7 0.0 collective-permute-done.6.refs_2_
  43.7 0.1 join_pieces.9
  43.8 4.0 %collective-permute-start.7 = (bf16[512,128]{1,0:T(8,128)(2,1)S(1)}, bf16[512,128]{1,0:T(8,128)(2,1)S(1)}, u32[]{:S(2)}, u32[]{:S(2)}) collective-permute-start(bf16[512,128]{1,0:T(8,128)(2,1)S(1)} %join_pieces.9), channel_id=1, source_target_pairs={{0,128},{1,385},{2,130},{3,387},{4,132},{5,389},{6,134},{7,391},{8... | collective-permute-start | bytes 393224 | tf_op jit(solution)/shard_map/ppermute | solution.py:263
  47.8 0.0 collective-permute-done.9.refs_2_
  47.8 0.1 join_pieces.11
  47.8 5.2 %collective-permute-start.10 = (bf16[512,128]{1,0:T(8,128)(2,1)S(1)}, bf16[512,128]{1,0:T(8,128)(2,1)S(1)}, u32[]{:S(2)}, u32[]{:S(2)}) collective-permute-start(bf16[512,128]{1,0:T(8,128)(2,1)S(1)} %join_pieces.11), channel_id=1, source_target_pairs={{0,384},{1,129},{2,386},{3,131},{4,388},{5,133},{6,390},{7,135},{8... | collective-permute-start | bytes 393224 | tf_op jit(solution)/shard_map/ppermute | solution.py:263
  53.1 0.0 copy-done
  53.1 0.2 fusion
  53.3 0.1 pad_add_fusion.place_ref
  53.4 0.0 collective-permute-done.2.refs_3_
  53.4 0.0 collective-permute-done.3.refs_4_
  53.4 3.0 %collective-permute-done.7.refs_5_ = bf16[512,128]{1,0:T(8,128)(2,1)S(1)} collective-permute-done((bf16[512,128]{1,0:T(8,128)(2,1)S(1)}, bf16[512,128]{1,0:T(8,128)(2,1)S(1)}, u32[]{:S(2)}, u32[]{:S(2)}) %collective-permute-start.7) | collective-permute-done | bytes 131104 | tf_op jit(solution)/shard_map/ppermute | solution.py:263
  56.4 8.4 %collective-permute-done.10.refs_6_ = bf16[512,128]{1,0:T(8,128)(2,1)S(1)} collective-permute-done((bf16[512,128]{1,0:T(8,128)(2,1)S(1)}, bf16[512,128]{1,0:T(8,128)(2,1)S(1)}, u32[]{:S(2)}, u32[]{:S(2)}) %collective-permute-start.10) | collective-permute-done | bytes 131104 | tf_op jit(solution)/shard_map/ppermute | solution.py:263
  64.8 0.1 join_all.1
  64.9 7.3 %all_gather.3.block_ref = bf16[512,512]{1,0:T(8,128)(2,1)S(1)} all-gather(bf16[512,128]{1,0:T(8,128)(2,1)S(1)} %join_all.1), channel_id=1, replica_groups={{0,1,2,3},{4,5,6,7},{8,9,10,11},{12,13,14,15},{16,17,18,19},{20,21,22,2..., dimensions={1}, use_global_device_ids=true | all-gather | bytes 655360 | tf_op jit(solution)/shard_map/all_gather | solution.py:304
  72.3 6.4 %block_roots.1 = (bf16[512,128]{1,0:T(8,128)(2,1)}, bf16[2,512,512]{2,1,0:T(8,128)(2,1)}) custom-call(s32[3]{0:T(128)S(1)} %pad_add_fusion.place_ref, bf16[512,512]{1,0:T(8,128)(2,1)S(1)} %all_gather.3.block_ref), custom_call_target="tpu_custom_call" | custom-call | flops 4160749568 | bytes 2097152 | tf_op jit(solution)/shard_map/block_roots/pallas_call | solution.py:139
  (2 shorter events, 0.1 us)
Async XLA Ops:
  3.0 50.1 %copy-start = (s32[1,8,2]{1,2,0:T(2,128)S(1)}, s32[1,8,2]{1,2,0:T(2,128)}, u32[]{:S(2)}) copy-start(s32[1,8,2]{1,2,0:T(2,128)} %param.3) | copy-start | bytes 196
  3.0 25.1 %collective-permute-start.4 = (bf16[1024,128]{1,0:T(8,128)(2,1)S(1)}, bf16[1024,128]{1,0:T(8,128)(2,1)S(1)}, u32[]{:S(2)}, u32[]{:S(2)}) collective-permute-start(bf16[1024,128]{1,0:T(8,128)(2,1)S(1)} %get-tuple-element.22), channel_id=1, source_target_pairs={{0,32},{1,481},{2,34},{3,483},{4,36},{5,485},{6,38},{7,487},{8,40}... | collective-permute-start | bytes 786440 | tf_op jit(solution)/shard_map/ppermute | solution.py:263
  15.0 19.2 %collective-permute-start.8 = (bf16[1024,128]{1,0:T(8,128)(2,1)S(1)}, bf16[1024,128]{1,0:T(8,128)(2,1)S(1)}, u32[]{:S(2)}, u32[]{:S(2)}) collective-permute-start(bf16[1024,128]{1,0:T(8,128)(2,1)S(1)} %get-tuple-element.26), channel_id=1, source_target_pairs={{0,480},{1,33},{2,482},{3,35},{4,484},{5,37},{6,486},{7,39},{8,488... | collective-permute-start | bytes 786440 | tf_op jit(solution)/shard_map/ppermute | solution.py:263
  16.9 19.3 %collective-permute-start = (bf16[1024,128]{1,0:T(8,128)(2,1)S(1)}, bf16[1024,128]{1,0:T(8,128)(2,1)S(1)}, u32[]{:S(2)}, u32[]{:S(2)}) collective-permute-start(bf16[1024,128]{1,0:T(8,128)(2,1)S(1)} %get-tuple-element.17), channel_id=1, source_target_pairs={{0,480},{1,33},{2,482},{3,35},{4,484},{5,37},{6,486},{7,39},{8,488... | collective-permute-start | bytes 786440 | tf_op jit(solution)/shard_map/ppermute | solution.py:263
  18.8 9.2 %collective-permute-start.5 = (bf16[512,128]{1,0:T(8,128)(2,1)S(1)}, bf16[512,128]{1,0:T(8,128)(2,1)S(1)}, u32[]{:S(2)}, u32[]{:S(2)}) collective-permute-start(bf16[512,128]{1,0:T(8,128)(2,1)S(1)} %get-tuple-element.24), channel_id=1, source_target_pairs={{0,64},{1,449},{2,66},{3,451},{4,68},{5,453},{6,70},{7,455},{8,72}... | collective-permute-start | bytes 393224 | tf_op jit(solution)/shard_map/ppermute | solution.py:263
  24.6 13.6 %collective-permute-start.1 = (bf16[1024,128]{1,0:T(8,128)(2,1)S(1)}, bf16[1024,128]{1,0:T(8,128)(2,1)S(1)}, u32[]{:S(2)}, u32[]{:S(2)}) collective-permute-start(bf16[1024,128]{1,0:T(8,128)(2,1)S(1)} %get-tuple-element.18), channel_id=1, source_target_pairs={{0,32},{1,481},{2,34},{3,483},{4,36},{5,485},{6,38},{7,487},{8,40}... | collective-permute-start | bytes 786440 | tf_op jit(solution)/shard_map/ppermute | solution.py:263
  28.2 15.6 %collective-permute-start.6 = (bf16[512,128]{1,0:T(8,128)(2,1)S(1)}, bf16[512,128]{1,0:T(8,128)(2,1)S(1)}, u32[]{:S(2)}, u32[]{:S(2)}) collective-permute-start(bf16[512,128]{1,0:T(8,128)(2,1)S(1)} %join_pieces.8), channel_id=1, source_target_pairs={{0,64},{1,449},{2,66},{3,451},{4,68},{5,453},{6,70},{7,455},{8,72}... | collective-permute-start | bytes 393224 | tf_op jit(solution)/shard_map/ppermute | solution.py:263
  34.3 13.5 %collective-permute-start.9 = (bf16[512,128]{1,0:T(8,128)(2,1)S(1)}, bf16[512,128]{1,0:T(8,128)(2,1)S(1)}, u32[]{:S(2)}, u32[]{:S(2)}) collective-permute-start(bf16[512,128]{1,0:T(8,128)(2,1)S(1)} %join_pieces.10), channel_id=1, source_target_pairs={{0,448},{1,65},{2,450},{3,67},{4,452},{5,69},{6,454},{7,71},{8,456... | collective-permute-start | bytes 393224 | tf_op jit(solution)/shard_map/ppermute | solution.py:263
  36.2 17.1 %collective-permute-start.2 = (bf16[512,128]{1,0:T(8,128)(2,1)S(1)}, bf16[512,128]{1,0:T(8,128)(2,1)S(1)}, u32[]{:S(2)}, u32[]{:S(2)}) collective-permute-start(bf16[512,128]{1,0:T(8,128)(2,1)S(1)} %join_pieces.6), channel_id=1, source_target_pairs={{0,448},{1,65},{2,450},{3,67},{4,452},{5,69},{6,454},{7,71},{8,456... | collective-permute-start | bytes 393224 | tf_op jit(solution)/shard_map/ppermute | solution.py:263
  38.2 15.1 %collective-permute-start.3 = (bf16[512,128]{1,0:T(8,128)(2,1)S(1)}, bf16[512,128]{1,0:T(8,128)(2,1)S(1)}, u32[]{:S(2)}, u32[]{:S(2)}) collective-permute-start(bf16[512,128]{1,0:T(8,128)(2,1)S(1)} %join_pieces.7), channel_id=1, source_target_pairs={{0,64},{1,449},{2,66},{3,451},{4,68},{5,453},{6,70},{7,455},{8,72}... | collective-permute-start | bytes 393224 | tf_op jit(solution)/shard_map/ppermute | solution.py:263
  43.8 12.6 %collective-permute-start.7 = (bf16[512,128]{1,0:T(8,128)(2,1)S(1)}, bf16[512,128]{1,0:T(8,128)(2,1)S(1)}, u32[]{:S(2)}, u32[]{:S(2)}) collective-permute-start(bf16[512,128]{1,0:T(8,128)(2,1)S(1)} %join_pieces.9), channel_id=1, source_target_pairs={{0,128},{1,385},{2,130},{3,387},{4,132},{5,389},{6,134},{7,391},{8... | collective-permute-start | bytes 393224 | tf_op jit(solution)/shard_map/ppermute | solution.py:263
  47.8 17.0 %collective-permute-start.10 = (bf16[512,128]{1,0:T(8,128)(2,1)S(1)}, bf16[512,128]{1,0:T(8,128)(2,1)S(1)}, u32[]{:S(2)}, u32[]{:S(2)}) collective-permute-start(bf16[512,128]{1,0:T(8,128)(2,1)S(1)} %join_pieces.11), channel_id=1, source_target_pairs={{0,384},{1,129},{2,386},{3,131},{4,388},{5,133},{6,390},{7,135},{8... | collective-permute-start | bytes 393224 | tf_op jit(solution)/shard_map/ppermute | solution.py:263

commit v8 on v6

--- a/solution.py
+++ b/solution.py
@@ -164,45 +164,48 @@
 
 OPPOSITE = "opposite"
 ROUTE = (
+    (-1, (-7, -5)),
     (1, (7, 5)),
-    (-1, (-7, -5)),
     OPPOSITE,
+    (1, (3, 1)),
     (-1, (-3, -1)),
-    (1, (3, 1)),
-    (2, (6,)),
     (-2, (-6,)),
+    (2, (6, 2)),
     (-2, (-2,)),
-    (2, (2,)),
+    (-4, (-4,)),
     (4, (4,)),
-    (-4, (-4,)),
 )
 
 
 def join_kernel(sums, parity_ref, *refs):
     *operands, out_ref = refs
-    rows = out_ref.shape[0]
-    summed = None
-    for operand, start, only in sums:
-        value = operands[operand][pl.ds(start, rows), :].astype(jnp.float32)
-        if only is not None:
-            value = jnp.where(parity_ref[0] == only, value, 0.0)
-        summed = value if summed is None else summed + value
-    out_ref[...] = summed.astype(jnp.bfloat16)
-
-
-def join(parity, rows, name, terms):
-    arrays = [term[0] for term in terms]
+    rows = out_ref.shape[0] // len(sums)
+    for order, terms in enumerate(sums):
+        summed = None
+        for operand, start, only in terms:
+            value = operands[operand][pl.ds(start, rows), :].astype(jnp.float32)
+            if only is not None:
+                value = jnp.where(parity_ref[0] == only, value, 0.0)
+            summed = value if summed is None else summed + value
+        out_ref[pl.ds(order * rows, rows), :] = summed.astype(jnp.bfloat16)
+
+
+def join(parity, rows, name, *sums):
+    arrays, plans = [], []
+    for terms in sums:
+        plans.append([(len(arrays) + k, *term[1:]) for k, term in enumerate(terms)])
+        arrays += [term[0] for term in terms]
     width = arrays[0].shape[1]
     vmem = pl.BlockSpec(memory_space=pltpu.VMEM)
     return pl.pallas_call(
-        functools.partial(join_kernel, [(k, *term[1:]) for k, term in enumerate(terms)]),
-        out_shape=jax.ShapeDtypeStruct((rows, width), jnp.bfloat16),
+        functools.partial(join_kernel, plans),
+        out_shape=jax.ShapeDtypeStruct((len(sums) * rows, width), jnp.bfloat16),
         in_specs=[pl.BlockSpec(memory_space=pltpu.SMEM)] + [vmem] * len(arrays),
         out_specs=vmem,
         compiler_params=pltpu.CompilerParams(vmem_limit_bytes=16 * 1024 * 1024),
         cost_estimate=pl.CostEstimate(
             flops=len(arrays) * rows * width,
-            bytes_accessed=2 * (len(arrays) + 1) * rows * width,
+            bytes_accessed=2 * (len(arrays) + len(sums)) * rows * width,
             transcendentals=0,
         ),
         name=name,
@@ -241,8 +244,7 @@
         if all(len(parts) == 1 for parts in leaving):
             value = jnp.concatenate([parts[0][0] for parts in leaving], 0)
         else:
-            (parts,) = leaving
-            value = join(parity, rows, "join_pieces", parts)
+            value = join(parity, rows, "join_pieces", *leaving)
         arrived = moved(value, lambda i, shift=shift: shift)
         for order, distance in enumerate(distances):
             terms[distance - shift].append((arrived, order * rows, None))

time: 74.2 us -> 76.3 us (1.028)
  the two profiles are of different devices: /device:TPU:41 before, /device:TPU:1 now
where the time goes in v8:
time: 76.3 us; the launch traced here: 75.9 us
  starting transfers between devices  40 us (52%)
  waiting for transfers between devices  18.2 us (24%)
  blocking collectives  7.31 us (10%)
  Pallas kernels  6.84 us (9%)
  local copies, waits for them, and re-layouts  2.05 us (3%)
  between operations  1.21 us (2%)
    ppermute x10, starting transfers between devices, moved(): return lax.ppermute(value, ('dp', 'work'), pairs)  40 us
    ppermute x10, waiting for transfers between devices, moved(): return lax.ppermute(value, ('dp', 'work'), pairs)  18.2 us
    all_gather x1, blocking collectives, local(): lax.all_gather(summed, 'work', axis=1, tiled=True, axis_index_groups=groups)  7.31 us
    pallas_call x1, Pallas kernels, block_call(): pl.pallas_call(block_kernel, out_shape=(jax.ShapeDtypeStruct((order, widt...  6.43 us
    squeeze x1, local copies, waits for them, and re-layouts, own(): lax.dynamic_index_in_dim(pieces, (place + side * distance) % size, 0, kee...  2.05 us
  transfers between devices with their start and end apart: 10, of which 4 were waited for; matrix products, arithmetic and copies ran while one was open for 0% of the time, Pallas kernels for 0%

profile of v8, /device:TPU:1, one launch (start us, length us, event | category | flops | bytes accessed | tf_op | source)
XLA Modules:
  0.0 75.9 jit_solution(9109544183951621001)
XLA Ops:
  1.0 2.0 %dynamic-slice_bitcast_fusion = (bf16[512,128]{1,0:T(8,128)(2,1)S(1)}, bf16[512,128]{1,0:T(8,128)(2,1)S(1)}, bf16[512,128]{1,0:T(8,128)(2,1)S(1)}, bf16[512,128]...) fusion(bf16[16,512,128]{2,1,0:T(8,128)(2,1)} %bitcast.36, ...), kind=kLoop, calls=%fused_computation.4 | loop fusion | bytes 4194368 | tf_op jit(solution)/shard_map/jit(dynamic_index_in_dim)/squeeze | solution.py:225
  3.1 12.0 %collective-permute-start = (bf16[1024,128]{1,0:T(8,128)(2,1)S(1)}, bf16[1024,128]{1,0:T(8,128)(2,1)S(1)}, u32[]{:S(2)}, u32[]{:S(2)}) collective-permute-start(bf16[1024,128]{1,0:T(8,128)(2,1)S(1)} %pad_maximum_fusion), channel_id=1, source_target_pairs={{0,32},{1,481},{2,34},{3,483},{4,36},{5,485},{6,38},{7,487},{8,40}... | collective-permute-start | bytes 786440 | tf_op jit(solution)/shard_map/ppermute | solution.py:233
  15.1 2.6 %collective-permute-start.2 = (bf16[1024,128]{1,0:T(8,128)(2,1)S(1)}, bf16[1024,128]{1,0:T(8,128)(2,1)S(1)}, u32[]{:S(2)}, u32[]{:S(2)}) collective-permute-start(bf16[1024,128]{1,0:T(8,128)(2,1)S(1)} %pad_maximum_fusion.2), channel_id=1, source_target_pairs={{0,32},{1,481},{2,34},{3,483},{4,36},{5,485},{6,38},{7,487},{8,40}... | collective-permute-start | bytes 786440 | tf_op jit(solution)/shard_map/ppermute | solution.py:233
  17.7 2.6 %collective-permute-start.6 = (bf16[1024,128]{1,0:T(8,128)(2,1)S(1)}, bf16[1024,128]{1,0:T(8,128)(2,1)S(1)}, u32[]{:S(2)}, u32[]{:S(2)}) collective-permute-start(bf16[1024,128]{1,0:T(8,128)(2,1)S(1)} %pad_maximum_fusion.3), channel_id=1, source_target_pairs={{0,480},{1,33},{2,482},{3,35},{4,484},{5,37},{6,486},{7,39},{8,488... | collective-permute-start | bytes 786440 | tf_op jit(solution)/shard_map/ppermute | solution.py:233
  20.4 3.1 %collective-permute-start.3 = (bf16[512,128]{1,0:T(8,128)(2,1)S(1)}, bf16[512,128]{1,0:T(8,128)(2,1)S(1)}, u32[]{:S(2)}, u32[]{:S(2)}) collective-permute-start(bf16[512,128]{1,0:T(8,128)(2,1)S(1)} %get-tuple-element.13), channel_id=1, source_target_pairs={{0,64},{1,449},{2,66},{3,451},{4,68},{5,453},{6,70},{7,455},{8,72}... | collective-permute-start | bytes 393224 | tf_op jit(solution)/shard_map/ppermute | solution.py:233
  23.5 0.0 copy-start
  23.5 1.9 %collective-permute-start.1 = (bf16[1024,128]{1,0:T(8,128)(2,1)S(1)}, bf16[1024,128]{1,0:T(8,128)(2,1)S(1)}, u32[]{:S(2)}, u32[]{:S(2)}) collective-permute-start(bf16[1024,128]{1,0:T(8,128)(2,1)S(1)} %pad_maximum_fusion.1), channel_id=1, source_target_pairs={{0,480},{1,33},{2,482},{3,35},{4,484},{5,37},{6,486},{7,39},{8,488... | collective-permute-start | bytes 786440 | tf_op jit(solution)/shard_map/ppermute | solution.py:233
  25.4 2.9 %collective-permute-done.3.refs_2_ = bf16[512,128]{1,0:T(8,128)(2,1)S(1)} collective-permute-done((bf16[512,128]{1,0:T(8,128)(2,1)S(1)}, bf16[512,128]{1,0:T(8,128)(2,1)S(1)}, u32[]{:S(2)}, u32[]{:S(2)}) %collective-permute-start.3) | collective-permute-done | bytes 131104 | tf_op jit(solution)/shard_map/ppermute | solution.py:233
  28.3 0.0 collective-permute-done.refs_4_.refs_1_
  28.3 0.0 collective-permute-done.2.refs_1_
  28.3 0.1 join_pieces.5
  28.4 3.0 %collective-permute-start.4 = (bf16[1024,128]{1,0:T(8,128)(2,1)S(1)}, bf16[1024,128]{1,0:T(8,128)(2,1)S(1)}, u32[]{:S(2)}, u32[]{:S(2)}) collective-permute-start(bf16[1024,128]{1,0:T(8,128)(2,1)S(1)} %join_pieces.5), channel_id=1, source_target_pairs={{0,64},{1,449},{2,66},{3,451},{4,68},{5,453},{6,70},{7,455},{8,72}... | collective-permute-start | bytes 786440 | tf_op jit(solution)/shard_map/ppermute | solution.py:233
  31.5 0.0 collective-permute-done.6.refs_1_
  31.5 0.1 join_pieces.7
  31.6 3.1 %collective-permute-start.7 = (bf16[512,128]{1,0:T(8,128)(2,1)S(1)}, bf16[512,128]{1,0:T(8,128)(2,1)S(1)}, u32[]{:S(2)}, u32[]{:S(2)}) collective-permute-start(bf16[512,128]{1,0:T(8,128)(2,1)S(1)} %join_pieces.7), channel_id=1, source_target_pairs={{0,448},{1,65},{2,450},{3,67},{4,452},{5,69},{6,454},{7,71},{8,456... | collective-permute-start | bytes 393224 | tf_op jit(solution)/shard_map/ppermute | solution.py:233
  34.7 0.0 collective-permute-done.1.refs_1_.refs_2_
  34.8 2.4 %collective-permute-start.5 = (bf16[512,128]{1,0:T(8,128)(2,1)S(1)}, bf16[512,128]{1,0:T(8,128)(2,1)S(1)}, u32[]{:S(2)}, u32[]{:S(2)}) collective-permute-start(bf16[512,128]{1,0:T(8,128)(2,1)S(1)} %join_pieces.6), channel_id=1, source_target_pairs={{0,448},{1,65},{2,450},{3,67},{4,452},{5,69},{6,454},{7,71},{8,456... | collective-permute-start | bytes 393224 | tf_op jit(solution)/shard_map/ppermute | solution.py:233
  37.2 9.0 %collective-permute-done.7.refs_2_ = bf16[512,128]{1,0:T(8,128)(2,1)S(1)} collective-permute-done((bf16[512,128]{1,0:T(8,128)(2,1)S(1)}, bf16[512,128]{1,0:T(8,128)(2,1)S(1)}, u32[]{:S(2)}, u32[]{:S(2)}) %collective-permute-start.7) | collective-permute-done | bytes 131104 | tf_op jit(solution)/shard_map/ppermute | solution.py:233
  46.2 0.1 join_pieces.8
  46.2 2.2 %collective-permute-start.8 = (bf16[512,128]{1,0:T(8,128)(2,1)S(1)}, bf16[512,128]{1,0:T(8,128)(2,1)S(1)}, u32[]{:S(2)}, u32[]{:S(2)}) collective-permute-start(bf16[512,128]{1,0:T(8,128)(2,1)S(1)} %join_pieces.8), channel_id=1, source_target_pairs={{0,384},{1,129},{2,386},{3,131},{4,388},{5,133},{6,390},{7,135},{8... | collective-permute-start | bytes 393224 | tf_op jit(solution)/shard_map/ppermute | solution.py:233
  48.4 0.0 collective-permute-done.4.refs_2_.refs_3_
  48.4 0.1 join_pieces.9
  48.5 7.0 %collective-permute-start.9 = (bf16[512,128]{1,0:T(8,128)(2,1)S(1)}, bf16[512,128]{1,0:T(8,128)(2,1)S(1)}, u32[]{:S(2)}, u32[]{:S(2)}) collective-permute-start(bf16[512,128]{1,0:T(8,128)(2,1)S(1)} %join_pieces.9), channel_id=1, source_target_pairs={{0,128},{1,385},{2,130},{3,387},{4,132},{5,389},{6,134},{7,391},{8... | collective-permute-start | bytes 393224 | tf_op jit(solution)/shard_map/ppermute | solution.py:233
  55.5 0.0 copy-done
  55.5 0.2 fusion
  55.7 0.1 pad_add_fusion.place_ref
  55.8 0.0 collective-permute-done.5.refs_4_
  55.8 0.9 %collective-permute-done.8.refs_5_ = bf16[512,128]{1,0:T(8,128)(2,1)S(1)} collective-permute-done((bf16[512,128]{1,0:T(8,128)(2,1)S(1)}, bf16[512,128]{1,0:T(8,128)(2,1)S(1)}, u32[]{:S(2)}, u32[]{:S(2)}) %collective-permute-start.8) | collective-permute-done | bytes 131104 | tf_op jit(solution)/shard_map/ppermute | solution.py:233
  56.7 5.3 %collective-permute-done.9.refs_6_ = bf16[512,128]{1,0:T(8,128)(2,1)S(1)} collective-permute-done((bf16[512,128]{1,0:T(8,128)(2,1)S(1)}, bf16[512,128]{1,0:T(8,128)(2,1)S(1)}, u32[]{:S(2)}, u32[]{:S(2)}) %collective-permute-start.9) | collective-permute-done | bytes 131104 | tf_op jit(solution)/shard_map/ppermute | solution.py:233
  62.1 0.1 join_all.1
  62.2 7.3 %all_gather.3.block_ref = bf16[512,512]{1,0:T(8,128)(2,1)S(1)} all-gather(bf16[512,128]{1,0:T(8,128)(2,1)S(1)} %join_all.1), channel_id=1, replica_groups={{0,1,2,3},{4,5,6,7},{8,9,10,11},{12,13,14,15},{16,17,18,19},{20,21,22,2..., dimensions={1}, use_global_device_ids=true | all-gather | bytes 655360 | tf_op jit(solution)/shard_map/all_gather | solution.py:263
  69.5 6.4 %block_roots.1 = (bf16[512,128]{1,0:T(8,128)(2,1)}, bf16[2,512,512]{2,1,0:T(8,128)(2,1)}) custom-call(s32[3]{0:T(128)S(1)} %pad_add_fusion.place_ref, bf16[512,512]{1,0:T(8,128)(2,1)S(1)} %all_gather.3.block_ref), custom_call_target="tpu_custom_call" | custom-call | flops 4160749568 | bytes 2097152 | tf_op jit(solution)/shard_map/block_roots/pallas_call | solution.py:139
  (5 shorter events, 0.1 us)
Async XLA Ops:
  3.1 25.3 %collective-permute-start = (bf16[1024,128]{1,0:T(8,128)(2,1)S(1)}, bf16[1024,128]{1,0:T(8,128)(2,1)S(1)}, u32[]{:S(2)}, u32[]{:S(2)}) collective-permute-start(bf16[1024,128]{1,0:T(8,128)(2,1)S(1)} %pad_maximum_fusion), channel_id=1, source_target_pairs={{0,32},{1,481},{2,34},{3,483},{4,36},{5,485},{6,38},{7,487},{8,40}... | collective-permute-start | bytes 786440 | tf_op jit(solution)/shard_map/ppermute | solution.py:233
  15.1 13.3 %collective-permute-start.2 = (bf16[1024,128]{1,0:T(8,128)(2,1)S(1)}, bf16[1024,128]{1,0:T(8,128)(2,1)S(1)}, u32[]{:S(2)}, u32[]{:S(2)}) collective-permute-start(bf16[1024,128]{1,0:T(8,128)(2,1)S(1)} %pad_maximum_fusion.2), channel_id=1, source_target_pairs={{0,32},{1,481},{2,34},{3,483},{4,36},{5,485},{6,38},{7,487},{8,40}... | collective-permute-start | bytes 786440 | tf_op jit(solution)/shard_map/ppermute | solution.py:233
  17.7 13.8 %collective-permute-start.6 = (bf16[1024,128]{1,0:T(8,128)(2,1)S(1)}, bf16[1024,128]{1,0:T(8,128)(2,1)S(1)}, u32[]{:S(2)}, u32[]{:S(2)}) collective-permute-start(bf16[1024,128]{1,0:T(8,128)(2,1)S(1)} %pad_maximum_fusion.3), channel_id=1, source_target_pairs={{0,480},{1,33},{2,482},{3,35},{4,484},{5,37},{6,486},{7,39},{8,488... | collective-permute-start | bytes 786440 | tf_op jit(solution)/shard_map/ppermute | solution.py:233
  20.4 8.0 %collective-permute-start.3 = (bf16[512,128]{1,0:T(8,128)(2,1)S(1)}, bf16[512,128]{1,0:T(8,128)(2,1)S(1)}, u32[]{:S(2)}, u32[]{:S(2)}) collective-permute-start(bf16[512,128]{1,0:T(8,128)(2,1)S(1)} %get-tuple-element.13), channel_id=1, source_target_pairs={{0,64},{1,449},{2,66},{3,451},{4,68},{5,453},{6,70},{7,455},{8,72}... | collective-permute-start | bytes 393224 | tf_op jit(solution)/shard_map/ppermute | solution.py:233
  23.5 32.1 %copy-start = (s32[1,8,2]{1,2,0:T(2,128)S(1)}, s32[1,8,2]{1,2,0:T(2,128)}, u32[]{:S(2)}) copy-start(s32[1,8,2]{1,2,0:T(2,128)} %param.3) | copy-start | bytes 196
  23.5 11.2 %collective-permute-start.1 = (bf16[1024,128]{1,0:T(8,128)(2,1)S(1)}, bf16[1024,128]{1,0:T(8,128)(2,1)S(1)}, u32[]{:S(2)}, u32[]{:S(2)}) collective-permute-start(bf16[1024,128]{1,0:T(8,128)(2,1)S(1)} %pad_maximum_fusion.1), channel_id=1, source_target_pairs={{0,480},{1,33},{2,482},{3,35},{4,484},{5,37},{6,486},{7,39},{8,488... | collective-permute-start | bytes 786440 | tf_op jit(solution)/shard_map/ppermute | solution.py:233
  28.4 20.0 %collective-permute-start.4 = (bf16[1024,128]{1,0:T(8,128)(2,1)S(1)}, bf16[1024,128]{1,0:T(8,128)(2,1)S(1)}, u32[]{:S(2)}, u32[]{:S(2)}) collective-permute-start(bf16[1024,128]{1,0:T(8,128)(2,1)S(1)} %join_pieces.5), channel_id=1, source_target_pairs={{0,64},{1,449},{2,66},{3,451},{4,68},{5,453},{6,70},{7,455},{8,72}... | collective-permute-start | bytes 786440 | tf_op jit(solution)/shard_map/ppermute | solution.py:233
  31.6 14.6 %collective-permute-start.7 = (bf16[512,128]{1,0:T(8,128)(2,1)S(1)}, bf16[512,128]{1,0:T(8,128)(2,1)S(1)}, u32[]{:S(2)}, u32[]{:S(2)}) collective-permute-start(bf16[512,128]{1,0:T(8,128)(2,1)S(1)} %join_pieces.7), channel_id=1, source_target_pairs={{0,448},{1,65},{2,450},{3,67},{4,452},{5,69},{6,454},{7,71},{8,456... | collective-permute-start | bytes 393224 | tf_op jit(solution)/shard_map/ppermute | solution.py:233
  34.8 21.0 %collective-permute-start.5 = (bf16[512,128]{1,0:T(8,128)(2,1)S(1)}, bf16[512,128]{1,0:T(8,128)(2,1)S(1)}, u32[]{:S(2)}, u32[]{:S(2)}) collective-permute-start(bf16[512,128]{1,0:T(8,128)(2,1)S(1)} %join_pieces.6), channel_id=1, source_target_pairs={{0,448},{1,65},{2,450},{3,67},{4,452},{5,69},{6,454},{7,71},{8,456... | collective-permute-start | bytes 393224 | tf_op jit(solution)/shard_map/ppermute | solution.py:233
  46.2 10.5 %collective-permute-start.8 = (bf16[512,128]{1,0:T(8,128)(2,1)S(1)}, bf16[512,128]{1,0:T(8,128)(2,1)S(1)}, u32[]{:S(2)}, u32[]{:S(2)}) collective-permute-start(bf16[512,128]{1,0:T(8,128)(2,1)S(1)} %join_pieces.8), channel_id=1, source_target_pairs={{0,384},{1,129},{2,386},{3,131},{4,388},{5,133},{6,390},{7,135},{8... | collective-permute-start | bytes 393224 | tf_op jit(solution)/shard_map/ppermute | solution.py:233
  48.5 13.6 %collective-permute-start.9 = (bf16[512,128]{1,0:T(8,128)(2,1)S(1)}, bf16[512,128]{1,0:T(8,128)(2,1)S(1)}, u32[]{:S(2)}, u32[]{:S(2)}) collective-permute-start(bf16[512,128]{1,0:T(8,128)(2,1)S(1)} %join_pieces.9), channel_id=1, source_target_pairs={{0,128},{1,385},{2,130},{3,387},{4,132},{5,389},{6,134},{7,391},{8... | collective-permute-start | bytes 393224 | tf_op jit(solution)/shard_map/ppermute | solution.py:233
